TPU v7x, 256 devices: a whole 4x4x8 slice. The times are simulated.
256 devices in a mesh: seq: 64 (over y_hi, x, z), head: 4 (over y_lo, core).
Axes of the slice: x: 4, y: 4 (y_hi: 2, y_lo: 2; y = y_hi * 2 + y_lo), z: 8, core: 2. Of those that a mesh axis runs over, the one named last changes fastest.
Arguments:
- video_query: bfloat16 [16384, 2048], P('seq', 'head'), may hold values from -360 to 360
- video_key: bfloat16 [16384, 2048], P('seq', 'head'), may hold values from -6 to 6
- video_value: bfloat16 [16384, 2048], P('seq', 'head'), may hold values from -6 to 6
- audio_query: bfloat16 [2048, 2048], P('seq', 'head'), may hold values from -360 to 360
- audio_key: bfloat16 [2048, 2048], P('seq', 'head'), may hold values from -6 to 6
- audio_value: bfloat16 [2048, 2048], P('seq', 'head'), may hold values from -6 to 6
- window_start: int32 [128], replicated, may hold values from 0 to 48, as said below
- video_out_weight: bfloat16 [2048, 4096], P('head'), may hold values from -0.125 to 0.125
- audio_out_weight: bfloat16 [2048, 2048], P('head'), may hold values from -0.125 to 0.125
Outputs:
- video_mixed: bfloat16 [16384, 4096], P(('seq', 'head'))
- audio_mixed: bfloat16 [2048, 2048], P(('seq', 'head'))
Inputs may be any that keep to these rules, and one draw needn't show every extreme that they name: Video block i (tokens i * 128 to (i + 1) * 128 - 1) is aligned with the 80 audio blocks of 16 tokens from window_start[i] on; every audio block is aligned with some video block.
All inputs are finite; a program needn't handle non-finite values.
Results may differ from a plain program's by a relative error of at most 0.02.
Values may be sent and summed in bfloat16 or wider, within the bound.
A program may use at most 128 MiB of HBM per device.

v0:
```python
import jax
import jax.numpy as jnp
from jax import lax
from jax.sharding import PartitionSpec as P

HEAD_DIM = 128
VBLOCK = 128
ABLOCK = 16


def head_scores(query_rows, key_rows, head_index):
    offset = head_index * HEAD_DIM
    head_query = lax.dynamic_slice_in_dim(query_rows, offset, HEAD_DIM, 1)
    head_key = lax.dynamic_slice_in_dim(key_rows, offset, HEAD_DIM, 1)
    scores = lax.dot_general(
        head_query, head_key, (((1,), (1,)), ((), ())), preferred_element_type=jnp.float32
    )
    return scores * HEAD_DIM ** (-0.5)


def shards(
    video_query,
    video_key,
    video_value,
    audio_query,
    audio_key,
    audio_value,
    window_start,
    video_out_weight,
    audio_out_weight,
):
    seq_count = lax.axis_size("seq")
    position = lax.axis_index("seq")
    vid_rows, local_feat = video_query.shape
    aud_rows = audio_query.shape[0]
    local_heads = local_feat // HEAD_DIM
    aud_total = aud_rows * seq_count
    window = 5 * (aud_total // ABLOCK) // 8
    vid_blocks = vid_rows // VBLOCK
    starts = lax.dynamic_slice_in_dim(window_start, position * vid_blocks, vid_blocks, 0)
    start_rows = jnp.repeat(starts, VBLOCK)
    audio_block = jnp.arange(aud_total, dtype=jnp.int32) // ABLOCK
    allowed = (audio_block[None, :] >= start_rows[:, None]) & (
        audio_block[None, :] < start_rows[:, None] + window
    )
    head_list = jnp.arange(local_heads, dtype=jnp.int32)
    all_key, all_value = (
        lax.all_gather(audio_key, "seq", axis=0, tiled=True),
        lax.all_gather(audio_value, "seq", axis=0, tiled=True),
    )

    def video_head(head_index):
        scores = head_scores(video_query, all_key, head_index)
        masked = jnp.where(allowed, scores, -jnp.inf)
        row_top = jnp.max(masked, axis=1, keepdims=True)
        weights = jnp.where(allowed, jnp.exp(masked - row_top), 0.0)
        total = jnp.sum(weights, axis=1, keepdims=True)
        head_value = lax.dynamic_slice_in_dim(all_value, head_index * HEAD_DIM, HEAD_DIM, 1)
        numerator = jnp.dot(
            weights.astype(jnp.bfloat16), head_value, preferred_element_type=jnp.float32
        )
        return numerator / total

    video_heads_out = lax.map(video_head, head_list)
    video_attention = (
        video_heads_out.transpose(1, 0, 2).reshape(vid_rows, local_feat).astype(jnp.bfloat16)
    )
    all_query = lax.all_gather(audio_query, "seq", axis=0, tiled=True)
    audio_allowed = allowed.T

    def audio_head_max(head_index):
        scores = head_scores(all_query, video_key, head_index)
        return jnp.max(jnp.where(audio_allowed, scores, -jnp.inf), axis=1)

    def audio_finish(head_index, scores, head_max):
        weights = jnp.where(audio_allowed, jnp.exp(scores - head_max[:, None]), 0.0)
        total = jnp.sum(weights, axis=1)
        head_value = lax.dynamic_slice_in_dim(video_value, head_index * HEAD_DIM, HEAD_DIM, 1)
        numerator = jnp.dot(
            weights.astype(jnp.bfloat16), head_value, preferred_element_type=jnp.float32
        )
        return (numerator, total)

    local_max = lax.map(audio_head_max, head_list)
    row_max = lax.pmax(local_max.astype(jnp.bfloat16), "seq").astype(local_max.dtype)
    numerators, totals = lax.map(
        lambda inputs: audio_finish(
            inputs[0], head_scores(all_query, video_key, inputs[0]), inputs[1]
        ),
        (head_list, row_max),
    )
    numer_rows = numerators.transpose(1, 0, 2).reshape(aud_total, local_feat)
    total_rows = totals.T
    numer_own, total_own = (
        lax.psum_scatter(numer_rows, "seq", scatter_dimension=0, tiled=True),
        lax.psum_scatter(total_rows, "seq", scatter_dimension=0, tiled=True),
    )
    audio_attention = (
        (numer_own.reshape(aud_rows, local_heads, HEAD_DIM) / total_own[:, :, None])
        .reshape(aud_rows, local_feat)
        .astype(jnp.bfloat16)
    )
    rows_here = video_attention
    video_mixed = lax.psum_scatter(
        jnp.dot(rows_here, video_out_weight, preferred_element_type=jnp.float32).astype(
            jnp.bfloat16
        ),
        "head",
        scatter_dimension=0,
        tiled=True,
    )
    rows_here = audio_attention
    audio_mixed = lax.psum_scatter(
        jnp.dot(rows_here, audio_out_weight, preferred_element_type=jnp.float32).astype(
            jnp.bfloat16
        ),
        "head",
        scatter_dimension=0,
        tiled=True,
    )
    return (video_mixed, audio_mixed)


def solution(mesh):
    in_specs = (
        P("seq", "head"),
        P("seq", "head"),
        P("seq", "head"),
        P("seq", "head"),
        P("seq", "head"),
        P("seq", "head"),
        P(),
        P("head", None),
        P("head", None),
    )
    out_specs = (P(("seq", "head"), None), P(("seq", "head"), None))
    return jax.shard_map(shards, mesh=mesh, in_specs=in_specs, out_specs=out_specs, check_vma=False)
```

profile of v0, /device:TPU:1, one launch (start us, length us, event | category | flops | bytes accessed | tf_op | source)
XLA Modules:
  0.0 1303.2 jit_solution(14906890700278388525)
XLA Ops:
  10.3 119.4 %all-gather.8.cloned.1.call-done = bf16[2048,512]{1,0:T(8,128)(2,1)} async-done(((bf16[32,512]{1,0:T(8,128)(2,1)}), bf16[2048,512]{1,0:T(8,128)(2,1)}) %all-gather.8.cloned.1.call-update) | async-done | bytes 2097168 | tf_op jit(solution)/shard_map/all_gather | solution.py:68
  129.8 12.0 while.39
  131.0 1.6 fusion.78
  134.0 1.6 fusion.78
  137.1 1.6 fusion.78
  140.1 1.6 fusion.78
  141.8 300.0 %pmax.7 = bf16[4,2048]{1,0:T(4,128)(2,1)S(1)} all-reduce(bf16[4,2048]{1,0:T(4,128)(2,1)S(1)} %get-tuple-element.120), channel_id=1, replica_groups=mesh['seq'=64,'head'=4] {'seq'}, use_global_device_ids=true, to_apply=%region_8.9 | all-reduce | flops 8192 | bytes 32768 | tf_op jit(solution)/shard_map/pmax | solution.py:85
  441.8 22.0 %while.40 = (s32[]{:T(128)}, f32[4,2048,128]{1,2,0:T(8,128)}, f32[4,2048]{1,0:T(4,128)S(1)}, s32[4]{0:T(128)S(1)}, bf16[2048,512]{1,0:T(8,128)(2,1)}, /*index=5*...) while((s32[]{:T(128)}, f32[4,2048,128]{1,2,0:T(8,128)}, ...), condition=%wide.region_11.12_spmd.clone.clone, body=%wide.region_9.11_spmd.clone.sunk.clone | while | flops 272627712 | bytes 3862203 | solution.py:86
  443.1 1.9 fusion.81
  445.0 2.2 fusion.82
  448.6 1.9 fusion.81
  450.5 2.2 fusion.82
  454.2 1.9 fusion.81
  456.1 2.2 fusion.82
  459.7 1.9 fusion.81
  461.6 2.2 fusion.82
  463.9 1.4 copy.18
  465.4 5.4 copy.16
  470.9 22.5 %while.38 = (s32[]{:T(128)}, bf16[4,256,128]{1,2,0:T(8,128)(2,1)S(1)}, s32[4]{0:T(128)S(1)}, bf16[256,512]{1,0:T(8,128)(2,1)}, bf16[2048,512]{1,0:T(8,128)(2,1)}...) while((s32[]{:T(128)}, ...), condition=%wide.region_3.4_spmd.clone.clone, body=%wide.region_0.3_spmd.clone.sunk.clone | while | flops 277937664 | bytes 7770279 | solution.py:64
  472.1 1.8 fusion.73
  474.6 1.8 fusion.75
  477.8 1.8 fusion.73
  480.2 1.8 fusion.75
  483.4 1.8 fusion.73
  485.8 1.8 fusion.75
  489.0 1.8 fusion.73
  491.5 1.8 fusion.75
  493.4 4.8 convolution_convert_fusion
  498.3 330.4 %reduce-scatter.15.cloned.1.call-done = f32[32,4]{1,0:T(8,128)} async-done(((f32[2048,4]{1,0:T(8,128)}), f32[32,4]{1,0:T(8,128)}) %reduce-scatter.15.cloned.1.call-update) | async-done | bytes 528
  829.5 368.8 %reduce-scatter.13.cloned.1.call-done = f32[32,512]{1,0:T(8,128)} async-done(((f32[2048,512]{1,0:T(8,128)}), f32[32,512]{1,0:T(8,128)}) %reduce-scatter.13.cloned.1.call-update) | async-done | bytes 65552
  1200.4 72.2 %reduce-scatter.9.cloned.1.call-done = bf16[64,4096]{1,0:T(8,128)(2,1)} async-done(((bf16[256,4096]{1,0:T(8,128)(2,1)}), bf16[64,4096]{1,0:T(8,128)(2,1)}) %reduce-scatter.9.cloned.1.call-update) | async-done | bytes 524304 | tf_op jit(solution)/shard_map/reduce_scatter | solution.py:104
  1272.6 23.8 %reduce-scatter.11.cloned.1.call-done = bf16[8,2048]{1,0:T(8,128)(2,1)} async-done(((bf16[32,2048]{1,0:T(8,128)(2,1)}), bf16[8,2048]{1,0:T(8,128)(2,1)}) %reduce-scatter.11.cloned.1.call-update) | async-done | bytes 32784 | tf_op jit(solution)/shard_map/reduce_scatter | solution.py:113
  (70 shorter events, 17.6 us)
Async XLA Ops:
  7.2 1192.1 %copy-start = (bf16[512,2048]{1,0:T(8,128)(2,1)S(1)}, bf16[512,2048]{1,0:T(8,128)(2,1)}, u32[]{:S(2)}) copy-start(bf16[512,2048]{1,0:T(8,128)(2,1)} %param.23) | copy-start | bytes 6291460
  7.2 122.6 %all-gather.8.cloned.1.call-start = ((), (), s32[]{:S(2)}) async-start(), calls=%async_computation.7 | async-start | bytes 2129920 | tf_op jit(solution)/shard_map/all_gather | solution.py:68
  7.9 462.9 %all-gather.4.cloned.1.call-start = ((), (), s32[]{:S(2)}) async-start(), calls=%async_computation.4 | async-start | bytes 2129920 | tf_op jit(solution)/shard_map/all_gather | solution.py:48
  8.7 462.2 %all-gather.6.cloned.1.call-start = ((), (), s32[]{:S(2)}) async-start(), calls=%async_computation.5 | async-start | bytes 2129920 | tf_op jit(solution)/shard_map/all_gather | solution.py:49
  9.4 819.3 %reduce-scatter.15.cloned.1.call-start = ((), (), s32[]{:S(2)}) async-start(), calls=%async_computation.10 | async-start | bytes 1064960
  465.3 732.9 %reduce-scatter.13.cloned.1.call-start = ((), (), s32[]{:S(2)}) async-start(), calls=%async_computation.9 | async-start | bytes 4259840
  470.8 801.8 %reduce-scatter.9.cloned.1.call-start = ((), (), s32[]{:S(2)}) async-start(), calls=%async_computation.6 | async-start | bytes 2621440 | tf_op jit(solution)/shard_map/reduce_scatter | solution.py:104
  498.2 798.2 %reduce-scatter.11.cloned.1.call-start = ((), (), s32[]{:S(2)}) async-start(), calls=%async_computation.8 | async-start | bytes 163840 | tf_op jit(solution)/shard_map/reduce_scatter | solution.py:113
Sparse Core Ops, SparseCore 0:
  11.7 117.9 all-gather.7
  133.5 114.4 all-gather.3
  251.7 114.5 all-gather.5
  465.4 363.1 reduce-scatter.14
  831.2 367.0 reduce-scatter.12
  1201.2 71.3 reduce-scatter.8
  1275.8 20.5 reduce-scatter.10
where the time goes:
time: 1300 us
  waiting for transfers between devices  917 us (71%)
  blocking collectives  300 us (23%)
  matrix products  43.1 us (3%)
  local copies, waits for them, and re-layouts  17.8 us (1%)
  between operations  14.2 us (1%)
    unnamed x9, waiting for transfers between devices  701 us
    pmax x1, blocking collectives, shards(): lax.pmax(local_max.astype(jnp.bfloat16), 'seq').astype(local_max.dtype)  300 us
    all_gather x1, waiting for transfers between devices, shards(): all_query = lax.all_gather(audio_query, 'seq', axis=0, tiled=True)  119 us
    reduce_scatter x1, waiting for transfers between devices, shards(): lax.psum_scatter(jnp.dot(rows_here, video_out_weight, preferred_element_t...  72.2 us
  transfers between devices with their start and end apart: 7, of which 5 were waited for; matrix products, arithmetic and copies ran while one was open for 5% of the time, Pallas kernels for 0%

commit v1 on v0

v1 whole, which is shorter than its diff:
```python
import math

import jax
import jax.numpy as jnp
from jax import lax
from jax.experimental import pallas as pl
from jax.experimental.pallas import tpu as pltpu
from jax.sharding import PartitionSpec as P

HD = 128
VB = 128
AB = 16
WIN = 80
NX, NZ = 4, 8
VR = 256
AR = 32
NEG = -1e30
C2 = math.log2(math.e) / math.sqrt(HD)
MESH = pl.DeviceIdType.MESH
F32, BF16 = jnp.float32, jnp.bfloat16


def dev(yh, x, z, yl, c):
    return ((yh * NX + x) * NZ + z, yl * 2 + c)


def nt(a, b):
    return lax.dot_general(a, b, (((1,), (1,)), ((), ())), preferred_element_type=F32)


def kernel(
    ws, vq_in, vk_in, vv_in, aq_in, ak_in, av_in, wv_in, wa_in, ov, oa,
    vq, vk, vv, aq, ak_flat, av_flat, wv, wa, kb, vo, va, po, pst, pr, prs, ao, aa, ysend, yrecv, yown, asend, arecv,
    s_pa, r_pa, s_pb, r_pb, s_z, r_z, s_f, r_f, s_vf, r_vf, s_w, r_w, s_vo, r_vo, s_p, r_p, s_ao, r_ao, s_y, r_y, s_ya, r_ya, l_w,
):
    seq, head = lax.axis_index("seq"), lax.axis_index("head")
    yh, x, z = seq // (NX * NZ), (seq // NZ) % NX, seq % NZ
    yl, c = head // 2, head % 2
    ak, av = (ref.reshape(2 * NX, NZ, AR, HD) for ref in (ak_flat, av_flat))
    is_self = yh == c
    core_peer = dev(yh, x, z, yl, 1 - c)
    yl_peer = dev(yh, x, z, 1 - yl, c)

    def peer(j):
        return dev(c, (x + j) % NX, z, yl, yh)

    def wait(ref, sem):
        pltpu.make_async_copy(ref, ref, sem).wait()

    own_w = [
        pltpu.make_async_copy(wv_in, wv.at[c], l_w.at[0]),
        pltpu.make_async_copy(wa_in, wa.at[c], l_w.at[1]),
    ]
    for copy in own_w:
        copy.start()

    barrier = pltpu.get_barrier_semaphore()

    def greet(device):
        pl.semaphore_signal(barrier, inc=1, device_id=device, device_id_type=MESH)

    for j in range(1, NX):
        greet(peer(j))

    @pl.when(jnp.logical_not(is_self))
    def _():
        greet(peer(0))

    for j in range(NX):
        greet(dev(1 - c, (x + j) % NX, z, yl, yh))
    for d in range(1, NZ):
        greet(dev(yh, x, (z + d) % NZ, yl, c))
    greet(core_peer)
    greet(yl_peer)
    pl.semaphore_wait(barrier, 2 * NX + NZ + 1 - is_self.astype(jnp.int32))

    def exchange(src, dst, send, recv, j):
        remote = pltpu.make_async_remote_copy(
            src_ref=src, dst_ref=dst, send_sem=send, recv_sem=recv, device_id=peer(j), device_id_type=MESH
        )
        if j:
            remote.start()
            return

        @pl.when(is_self)
        def _():
            pltpu.make_async_copy(src, dst, recv).start()

        @pl.when(jnp.logical_not(is_self))
        def _():
            remote.start()

    def cols(j):
        return pl.ds(pl.multiple_of(((x + j) % NX) * HD, HD), HD)

    here = yh * NX + x
    for j in range(NX):
        exchange(aq_in.at[:, cols(j)], aq.at[z, x], s_pa.at[0, j], r_pa.at[0, x], j)
        exchange(ak_in.at[:, cols(j)], ak.at[here, z], s_pa.at[1, j], r_pa.at[1, x], j)
        exchange(av_in.at[:, cols(j)], av.at[here, z], s_pa.at[2, j], r_pa.at[2, x], j)
    for t, (src, dst) in enumerate(((vk_in, vk.at[yh]), (vv_in, vv.at[yh]), (vq_in, vq))):
        for j in range(NX):
            exchange(src.at[:, cols(j)], dst.at[x], s_pb.at[t, j], r_pb.at[t, x], j)

    other_w = [
        pltpu.make_async_remote_copy(
            src_ref=src, dst_ref=dst.at[c], send_sem=s_w.at[t], recv_sem=r_w.at[t],
            device_id=core_peer, device_id_type=MESH,
        )
        for t, (src, dst) in enumerate(((wv_in, wv), (wa_in, wa)))
    ]
    for copy in other_w:
        copy.start()

    lane = lax.broadcasted_iota(jnp.int32, (VB, 128), 1)
    for a in range(2):
        for xs in range(NX):
            for i in range(2):
                start = ws[((a * NX + xs) * NZ + z) * 2 + i]
                inside = (lane >= start) & (lane < start + WIN)
                kb[a, xs, pl.ds(i * VB, VB), :] = jnp.where(inside, 0.0, NEG).astype(BF16)

    for xs in range(NX):
        wait(aq.at[z, xs], r_pa.at[0, xs])
        wait(ak.at[c * NX + xs, z], r_pa.at[1, xs])
        wait(av.at[c * NX + xs, z], r_pa.at[2, xs])

    half = pl.ds(c * NX, NX)
    other_half = pl.ds((1 - c) * NX, NX)

    def chunk(t, zz):
        return aq.at[zz] if t == 0 else (ak, av)[t - 1].at[half, zz]

    def forward(zz):
        for t in (1, 2):
            pltpu.make_async_remote_copy(
                src_ref=chunk(t, zz), dst_ref=chunk(t, zz), send_sem=s_f.at[t - 1, zz], recv_sem=r_f.at[t - 1, zz],
                device_id=core_peer, device_id_type=MESH,
            ).start()

    forward(z)
    sent = []
    for k in range(1, NZ // 2 + 1):
        hops = [(0, t) for t in range(3)] + [(1, t) for t in range(3)]
        if k == NZ // 2:
            hops = [(0, 0), (0, 1), (1, 2)]
        for way, t in hops:
            zz = (z - k + 1 + NZ) % NZ if way == 0 else (z + k - 1) % NZ
            to = (z + 1) % NZ if way == 0 else (z + NZ - 1) % NZ
            copy = pltpu.make_async_remote_copy(
                src_ref=chunk(t, zz), dst_ref=chunk(t, zz), send_sem=s_z.at[way, t, k - 1], recv_sem=r_z.at[way, t, k - 1],
                device_id=dev(yh, x, to, yl, c), device_id_type=MESH,
            )
            copy.start()
            sent.append(copy)
        for way, t in hops:
            zz = (z - k + NZ) % NZ if way == 0 else (z + k) % NZ
            wait(chunk(t, zz), r_z.at[way, t, k - 1])
        if k < NZ // 2:
            forward((z - k + NZ) % NZ)
            forward((z + k) % NZ)
        else:
            forward((z + k) % NZ)

    vf = []
    for t, ref in enumerate((vk, vv)):
        for xs in range(NX):
            wait(ref.at[c, xs], r_pb.at[t, xs])
        copy = pltpu.make_async_remote_copy(
            src_ref=ref.at[c], dst_ref=ref.at[c], send_sem=s_vf.at[t], recv_sem=r_vf.at[t],
            device_id=core_peer, device_id_type=MESH,
        )
        copy.start()
        vf.append(copy)
    for xs in range(NX):
        wait(vq.at[xs], r_pb.at[2, xs])

    def late(zz, carry):
        wait(ak.at[other_half, zz], r_f.at[0, zz])
        wait(av.at[other_half, zz], r_f.at[1, zz])
        return carry

    lax.fori_loop(0, NZ, late, 0)

    ones_win = jnp.ones((WIN * AB, HD), BF16)

    def video_block(n, carry):
        xs, i = n // 2, n % 2
        start = ws[((c * NX + xs) * NZ + z) * 2 + i]
        blocks = pl.ds(start, WIN)
        q = vq[xs, pl.ds(pl.multiple_of(i * VB, VB), VB), :]
        s = nt(q, ak_flat[blocks].reshape(WIN * AB, HD))
        top = jnp.max(s, axis=1, keepdims=True)
        p = jnp.exp2((s - top) * C2).astype(BF16)
        v = jnp.concatenate([av_flat[blocks].reshape(WIN * AB, HD), ones_win], axis=1)
        o = jnp.dot(p, v, preferred_element_type=F32)
        vo[xs, i] = (o[:, :HD] / o[:, HD:]).astype(BF16).reshape(2, VB // 2, HD)
        return carry

    lax.fori_loop(0, 2 * NX, video_block, 0)

    my_slot = yh * NX + x

    def vo_copy(j, k):
        return pltpu.make_async_remote_copy(
            src_ref=vo.at[(x + j) % NX, :, k], dst_ref=va.at[my_slot], send_sem=s_vo.at[j, k], recv_sem=r_vo.at[my_slot],
            device_id=dev(c, (x + j) % NX, z, yl, k), device_id_type=MESH,
        )

    for j in range(NX):
        for k in range(2):
            copy = vo_copy(j, k)
            if j:
                copy.start()
            else:
                to_self = is_self & (c == k)

                @pl.when(to_self)
                def _(k=k):
                    pltpu.make_async_copy(vo.at[x, :, k], va.at[my_slot], r_vo.at[my_slot]).start()

                @pl.when(jnp.logical_not(to_self))
                def _(copy=copy):
                    copy.start()

    for t, ref in enumerate((vk, vv)):
        wait(ref.at[1 - c], r_vf.at[t])
    row = lax.broadcasted_iota(jnp.int32, (2 * NX * AR, 128), 0)
    lane2 = lax.broadcasted_iota(jnp.int32, (2 * NX * AR, 128), 1)
    x_of, b_of, u_of = (row // AR) % NX, (row % AR) // AB, row // (NX * AR)
    eye = lax.broadcasted_iota(jnp.int32, (HD, HD), 0) == lax.broadcasted_iota(jnp.int32, (HD, HD), 1)
    ones_vid = jnp.ones((2 * NX * VR, HD), BF16)

    def audio_pair(it, carry):
        z0, z1 = (z + 2 * it) % NZ, (z + 2 * it + 1) % NZ
        q = jnp.concatenate([aq[z0].reshape(NX * AR, HD), aq[z1].reshape(NX * AR, HD)], axis=0)
        zz = (z + 2 * it + u_of) % NZ
        block = ((c * NX + x_of) * NZ + zz) * 2 + b_of
        q = jnp.concatenate([q, jnp.where(lane2 == block, 1.0, 0.0).astype(BF16)], axis=1)
        key = jnp.concatenate([vk[...].reshape(2 * NX * VR, HD), kb[...].reshape(2 * NX * VR, HD)], axis=1)
        s = nt(q, key)
        top = jnp.max(s, axis=1, keepdims=True)
        p = jnp.exp2((s - top) * C2).astype(BF16)
        v = jnp.concatenate([vv[...].reshape(2 * NX * VR, HD), ones_vid], axis=1)
        o = jnp.dot(p, v, preferred_element_type=F32)
        part = (o[:, :HD] / o[:, HD:]).astype(BF16)
        level = top * C2 + jnp.log2(o[:, HD:])
        for u in range(2):
            d = 2 * it + u
            rows = slice(u * NX * AR, (u + 1) * NX * AR)
            flat = jnp.sum(jnp.where(eye, level[rows], 0.0), axis=0, keepdims=True)
            flat = jnp.broadcast_to(flat, (8, HD))

            def keep(d=d, rows=rows, flat=flat):
                po[d] = part[rows]
                pst[d] = flat
                slot = NZ - d
                to = dev(yh, x, (z + d) % NZ, yl, c)
                for t, (src, dst) in enumerate(((po, pr), (pst, prs))):
                    pltpu.make_async_remote_copy(
                        src_ref=src.at[d], dst_ref=dst.at[slot], send_sem=s_p.at[t, d], recv_sem=r_p.at[t, slot],
                        device_id=to, device_id_type=MESH,
                    ).start()

            if u:
                keep()
            else:

                @pl.when(it == 0)
                def _(rows=rows, flat=flat):
                    pr[0] = part[rows]
                    prs[0] = flat

                pl.when(it > 0)(keep)
        return carry

    lax.fori_loop(0, NZ // 2, audio_pair, 0)

    for copy in own_w:
        copy.wait()
    for t, ref in enumerate((wv, wa)):
        wait(ref.at[1 - c], r_w.at[t])
    for h in range(2 * NX):
        wait(va.at[h], r_vo.at[h])
    xv = jnp.concatenate(
        [
            jnp.concatenate([va[h, 1 - yl] for h in range(2 * NX)], axis=1),
            jnp.concatenate([va[h, yl] for h in range(2 * NX)], axis=1),
        ],
        axis=0,
    )
    n_chunks = ysend.shape[0]
    width = ysend.shape[2]

    def y_copy(n):
        return pltpu.make_async_remote_copy(
            src_ref=ysend.at[n], dst_ref=yrecv.at[n], send_sem=s_y.at[n], recv_sem=r_y.at[n],
            device_id=yl_peer, device_id_type=MESH,
        )

    def project(n, carry):
        at = pl.ds(pl.multiple_of(n * width, width), width)
        w = jnp.concatenate([wv[0, :, at], wv[1, :, at]], axis=0)
        y = jnp.dot(xv, w, preferred_element_type=F32)
        ysend[n] = y[: VB // 2].astype(BF16)
        yown[n] = y[VB // 2 :]
        y_copy(n).start()
        return carry

    lax.fori_loop(0, n_chunks, project, 0)

    for d in range(1, NZ):
        wait(pr.at[d], r_p.at[0, d])
        wait(prs.at[d], r_p.at[1, d])
    levels = jnp.concatenate([prs[d, 0:1, :] for d in range(NZ)], axis=0)
    share = jnp.exp2(levels - jnp.max(levels, axis=0, keepdims=True))
    share = share / jnp.sum(share, axis=0, keepdims=True)
    share = jnp.transpose(jnp.concatenate([share, jnp.zeros((HD - NZ, HD), F32)], axis=0))
    mixed = share[:, 0:1] * pr[0].astype(F32)
    for d in range(1, NZ):
        mixed = mixed + share[:, d : d + 1] * pr[d].astype(F32)
    mixed = mixed.reshape(NX, 2, 2, 8, HD)
    for k in range(2):
        ao[k] = mixed[:, :, k].reshape(NX, 16, HD).astype(BF16)
    for j in range(NX):
        for k in range(2):
            copy = pltpu.make_async_remote_copy(
                src_ref=ao.at[k, (x + j) % NX], dst_ref=aa.at[my_slot], send_sem=s_ao.at[j, k], recv_sem=r_ao.at[my_slot],
                device_id=dev(c, (x + j) % NX, z, yl, k), device_id_type=MESH,
            )
            if j:
                copy.start()
            else:
                to_self = is_self & (c == k)

                @pl.when(to_self)
                def _(k=k):
                    pltpu.make_async_copy(ao.at[k, x], aa.at[my_slot], r_ao.at[my_slot]).start()

                @pl.when(jnp.logical_not(to_self))
                def _(copy=copy):
                    copy.start()

    def finish(n, carry):
        y_copy(n).wait_recv()
        at = pl.ds(pl.multiple_of(n * width, width), width)
        ov[:, at] = (yown[n] + yrecv[n].astype(F32)).astype(BF16)
        return carry

    lax.fori_loop(0, n_chunks, finish, 0)

    for h in range(2 * NX):
        wait(aa.at[h], r_ao.at[h])
    xa = jnp.concatenate([aa[h] for h in range(2 * NX)], axis=1)
    for n in range(wa.shape[2] // 512):
        at = slice(n * 512, (n + 1) * 512)
        w = jnp.concatenate([wa[0, :, at], wa[1, :, at]], axis=0)
        asend[:, :, at] = jnp.dot(xa, w, preferred_element_type=F32).reshape(2, 8, 512)
    last = pltpu.make_async_remote_copy(
        src_ref=asend.at[1 - yl], dst_ref=arecv, send_sem=s_ya, recv_sem=r_ya, device_id=yl_peer, device_id_type=MESH
    )
    last.start()
    last.wait_recv()
    oa[...] = (asend[yl] + arecv[...]).astype(BF16)

    last.wait_send()
    for copy in other_w + vf + sent:
        copy.wait_send()

    def y_sent(n, carry):
        y_copy(n).wait_send()
        return carry

    lax.fori_loop(0, n_chunks, y_sent, 0)

    def f_sent(zz, carry):
        wait(ak.at[half, zz], s_f.at[0, zz])
        wait(av.at[half, zz], s_f.at[1, zz])
        return carry

    lax.fori_loop(0, NZ, f_sent, 0)
    for d in range(1, NZ):
        wait(po.at[d], s_p.at[0, d])
        wait(pst.at[d], s_p.at[1, d])

    def sent_exchange(j):
        for t in range(3):
            wait(aq.at[z, x], s_pa.at[t, j])
            wait(vq.at[x], s_pb.at[t, j])

    for j in range(1, NX):
        sent_exchange(j)

    @pl.when(jnp.logical_not(is_self))
    def _():
        sent_exchange(0)

    for j in range(NX):
        for k in range(2):

            def done(j=j, k=k):
                wait(va.at[my_slot], s_vo.at[j, k])
                wait(aa.at[my_slot], s_ao.at[j, k])

            if j:
                done()
            else:
                pl.when(jnp.logical_not(is_self & (c == k)))(done)


def shards(vq, vk, vv, aq, ak, av, ws, wv, wa):
    n_chunks = 8
    dv, da = wv.shape[1], wa.shape[1]
    dma = pltpu.SemaphoreType.DMA
    vmem = pltpu.VMEM
    scratch = [
        vmem((NX, VR, HD), BF16),
        vmem((2, NX, VR, HD), BF16),
        vmem((2, NX, VR, HD), BF16),
        vmem((NZ, NX, AR, HD), BF16),
        vmem((2 * NX * NZ * AR // AB, AB, HD), BF16),
        vmem((2 * NX * NZ * AR // AB, AB, HD), BF16),
        vmem((2,) + wv.shape, BF16),
        vmem((2,) + wa.shape, BF16),
        vmem((2, NX, VR, HD), BF16),
        vmem((NX, 2, 2, VB // 2, HD), BF16),
        vmem((2 * NX, 2, VB // 2, HD), BF16),
        vmem((NZ, NX * AR, HD), BF16),
        vmem((NZ, 8, HD), F32),
        vmem((NZ, NX * AR, HD), BF16),
        vmem((NZ, 8, HD), F32),
        vmem((2, NX, 16, HD), BF16),
        vmem((2 * NX, 16, HD), BF16),
        vmem((n_chunks, VB // 2, dv // n_chunks), BF16),
        vmem((n_chunks, VB // 2, dv // n_chunks), BF16),
        vmem((n_chunks, VB // 2, dv // n_chunks), F32),
        vmem((2, 8, da), F32),
        vmem((8, da), F32),
        dma((3, NX)), dma((3, NX)),
        dma((3, NX)), dma((3, NX)),
        dma((2, 3, NZ // 2)), dma((2, 3, NZ // 2)),
        dma((2, NZ)), dma((2, NZ)),
        dma((2,)), dma((2,)),
        dma((2,)), dma((2,)),
        dma((NX, 2)), dma((2 * NX,)),
        dma((2, NZ)), dma((2, NZ)),
        dma((NX, 2)), dma((2 * NX,)),
        dma((n_chunks,)), dma((n_chunks,)),
        dma, dma,
        dma((2,)),
    ]
    any_spec = pl.BlockSpec(memory_space=pl.ANY)
    return pl.pallas_call(
        kernel,
        out_shape=(
            jax.ShapeDtypeStruct((vq.shape[0] // 4, dv), BF16),
            jax.ShapeDtypeStruct((aq.shape[0] // 4, da), BF16),
        ),
        in_specs=[pl.BlockSpec(memory_space=pltpu.SMEM)] + [any_spec] * 8,
        out_specs=(pl.BlockSpec(memory_space=pltpu.VMEM), pl.BlockSpec(memory_space=pltpu.VMEM)),
        scratch_shapes=scratch,
        compiler_params=pltpu.CompilerParams(
            collective_id=0, has_side_effects=True, vmem_limit_bytes=48 * 1024 * 1024
        ),
        cost_estimate=pl.CostEstimate(flops=3_000_000_000, bytes_accessed=16_000_000, transcendentals=4_000_000),
    )(ws, vq, vk, vv, aq, ak, av, wv, wa)


def solution(mesh):
    part = P("seq", "head")
    in_specs = (part, part, part, part, part, part, P(), P("head", None), P("head", None))
    out_specs = (P(("seq", "head"), None), P(("seq", "head"), None))
    return jax.shard_map(shards, mesh=mesh, in_specs=in_specs, out_specs=out_specs, check_vma=False)
```

time: 1300 us -> 76.7 us (0.06)
  waiting for transfers between devices: 917 us -> 0 us
  blocking collectives: 300 us -> 0 us
  Pallas kernels: 0 us -> 66.9 us
  matrix products: 43.1 us -> 0 us
  between operations: 14.2 us -> 0.66 us
    unnamed x9 -> x0, waiting for transfers between devices: 701 us -> none
    pmax x1 -> x0, blocking collectives: 300 us -> none  [shards(): lax.pmax(local_max.astype(jnp.bfloat16), 'seq').astype(local_max.dtype)]
    all_gather x3 -> x0, waiting for transfers between devices: 119 us -> none  [the longest x1 119 us: shards(): all_query = lax.all_gather(audio_query, 'seq', axis=0, tiled=True)]
    reduce_scatter x2 -> x0, waiting for transfers between devices: 96 us -> none  [the longest x1 72.2 us: shards(): lax.psum_scatter(jnp.dot(rows_here, video_out_weight, preferred_element_t...]
    pallas_call x0 -> x1, Pallas kernels: none -> 66.9 us  [shards(): pl.pallas_call(kernel, out_shape=(jax.ShapeDtypeStruct((vq.shape[0] // 4,...]
    dot_general x22 -> x0, matrix products: 43.1 us -> none  [the longest x12 21.2 us: head_scores(): lax.dot_general(head_query, head_key, (((1,), (1,)), ((), ())), preferred...]
  transfers between devices with their start and end apart: 7 -> 0, of which waited for: 5 -> 0; matrix products, arithmetic and copies ran while one was open for 5% -> 0% of each run, Pallas kernels for 0% -> 0%
where the time goes in v1:
time: 76.7 us; the launch traced here: 76.3 us
  Pallas kernels  66.9 us (87%)
  local copies, waits for them, and re-layouts  8.77 us (11%)
    pallas_call x1, Pallas kernels, shards(): pl.pallas_call(kernel, out_shape=(jax.ShapeDtypeStruct((vq.shape[0] // 4,...  66.9 us
    unnamed x18, local copies, waits for them, and re-layouts  8.77 us

profile of v1, /device:TPU:1, one launch (start us, length us, event | category | flops | bytes accessed | tf_op | source)
XLA Modules:
  0.0 76.3 jit_solution(15222398288126776332)
XLA Ops:
  0.6 0.0 copy-start
  0.6 1.6 %copy-done = bf16[512,2048]{1,0:T(8,128)(2,1)S(1)} copy-done((bf16[512,2048]{1,0:T(8,128)(2,1)S(1)}, bf16[512,2048]{1,0:T(8,128)(2,1)}, u32[]{:S(2)}) %copy-start) | copy-done | bytes 2097176
  2.2 0.0 copy-start.1
  2.2 0.9 %copy-done.1 = bf16[256,512]{1,0:T(8,128)(2,1)S(1)} copy-done((bf16[256,512]{1,0:T(8,128)(2,1)S(1)}, bf16[256,512]{1,0:T(8,128)(2,1)}, u32[]{:S(2)}) %copy-start.1) | copy-done | bytes 262168
  3.2 0.0 copy-start.2
  3.2 0.9 %copy-done.2 = bf16[256,512]{1,0:T(8,128)(2,1)S(1)} copy-done((bf16[256,512]{1,0:T(8,128)(2,1)S(1)}, bf16[256,512]{1,0:T(8,128)(2,1)}, u32[]{:S(2)}) %copy-start.2) | copy-done | bytes 262168
  4.1 0.0 copy-start.3
  4.1 0.9 %copy-done.3 = bf16[256,512]{1,0:T(8,128)(2,1)S(1)} copy-done((bf16[256,512]{1,0:T(8,128)(2,1)S(1)}, bf16[256,512]{1,0:T(8,128)(2,1)}, u32[]{:S(2)}) %copy-start.3) | copy-done | bytes 262168
  5.1 0.0 copy-start.4
  5.1 0.8 copy-done.4
  5.8 0.0 copy-start.5
  5.8 0.8 copy-done.5
  6.6 0.0 copy-start.6
  6.6 0.8 copy-done.6
  7.4 0.0 copy-start.7
  7.4 0.7 copy-done.7
  8.0 66.9 %shard_map.104 = (bf16[64,4096]{1,0:T(8,128)(2,1)S(1)}, bf16[8,2048]{1,0:T(8,128)(2,1)S(1)}) custom-call(s32[128]{0:T(128)S(1)} %copy-done.7, bf16[256,512]{1,0:T(8,128)(2,1)S(1)} %copy-done.1, bf16[256,512]{1,0:T(8,128)(2,1)S(1)} %copy-done.2, bf16[256,512]{1,0:T(8,128)(2,1)S(1)} %copy-done.3, bf16[32,512]{1,0:T(8,128)(2,1)S(1)} %copy-done.4, ...), custom_call_target="tpu_custom_call" | custom-call | flops 3000000000 | bytes 16000000 | tf_op jit(solution)/shard_map/pallas_call | solution.py:453
  74.9 0.8 %copy.13 = bf16[64,4096]{1,0:T(8,128)(2,1)} copy(bf16[64,4096]{1,0:T(8,128)(2,1)S(1)} %get-tuple-element.4) | data formatting | bytes 1048576
  75.7 0.6 copy.14
Async XLA Ops:
  0.6 1.6 %copy-start = (bf16[512,2048]{1,0:T(8,128)(2,1)S(1)}, bf16[512,2048]{1,0:T(8,128)(2,1)}, u32[]{:S(2)}) copy-start(bf16[512,2048]{1,0:T(8,128)(2,1)} %wa_in.1) | copy-start | bytes 6291460
  2.2 0.9 %copy-start.1 = (bf16[256,512]{1,0:T(8,128)(2,1)S(1)}, bf16[256,512]{1,0:T(8,128)(2,1)}, u32[]{:S(2)}) copy-start(bf16[256,512]{1,0:T(8,128)(2,1)} %vq_in.1) | copy-start | bytes 786436
  3.2 0.9 %copy-start.2 = (bf16[256,512]{1,0:T(8,128)(2,1)S(1)}, bf16[256,512]{1,0:T(8,128)(2,1)}, u32[]{:S(2)}) copy-start(bf16[256,512]{1,0:T(8,128)(2,1)} %vk_in.1) | copy-start | bytes 786436
  4.1 0.9 %copy-start.3 = (bf16[256,512]{1,0:T(8,128)(2,1)S(1)}, bf16[256,512]{1,0:T(8,128)(2,1)}, u32[]{:S(2)}) copy-start(bf16[256,512]{1,0:T(8,128)(2,1)} %vv_in.1) | copy-start | bytes 786436
  5.1 0.8 copy-start.4
  5.8 0.8 copy-start.5
  6.6 0.8 copy-start.6
  7.4 0.7 copy-start.7

commit v2 on v1

--- a/solution.py
+++ b/solution.py
@@ -40,9 +40,12 @@
     is_self = yh == c
     core_peer = dev(yh, x, z, yl, 1 - c)
     yl_peer = dev(yh, x, z, 1 - yl, c)
+    cross_peer = dev(1 - yh, x, z, 1 - yl, c)
 
     def peer(j):
         return dev(c, (x + j) % NX, z, yl, yh)
+
+    drains = []
 
     def wait(ref, sem):
         pltpu.make_async_copy(ref, ref, sem).wait()
@@ -59,20 +62,14 @@
     def greet(device):
         pl.semaphore_signal(barrier, inc=1, device_id=device, device_id_type=MESH)
 
-    for j in range(1, NX):
-        greet(peer(j))
-
-    @pl.when(jnp.logical_not(is_self))
-    def _():
-        greet(peer(0))
-
-    for j in range(NX):
-        greet(dev(1 - c, (x + j) % NX, z, yl, yh))
+    group = [(p, j, q) for p in range(2) for j in range(NX) for q in range(2) if p or j or q]
+    for p, j, q in group:
+        greet(dev((yh + p) % 2, (x + j) % NX, z, yl, (c + q) % 2))
     for d in range(1, NZ):
         greet(dev(yh, x, (z + d) % NZ, yl, c))
-    greet(core_peer)
     greet(yl_peer)
-    pl.semaphore_wait(barrier, 2 * NX + NZ + 1 - is_self.astype(jnp.int32))
+    greet(cross_peer)
+    pl.semaphore_wait(barrier, len(group) + NZ + 1)
 
     def exchange(src, dst, send, recv, j):
         remote = pltpu.make_async_remote_copy(
@@ -101,6 +98,18 @@
     for t, (src, dst) in enumerate(((vk_in, vk.at[yh]), (vv_in, vv.at[yh]), (vq_in, vq))):
         for j in range(NX):
             exchange(src.at[:, cols(j)], dst.at[x], s_pb.at[t, j], r_pb.at[t, x], j)
+
+    def exchange_sent():
+        def one(j):
+            for t in range(3):
+                wait(aq.at[z, x], s_pa.at[t, j])
+                wait(vq.at[x], s_pb.at[t, j])
+
+        for j in range(1, NX):
+            one(j)
+        pl.when(jnp.logical_not(is_self))(lambda: one(0))
+
+    drains.append(exchange_sent)
 
     other_w = [
         pltpu.make_async_remote_copy(
@@ -112,6 +121,8 @@
     for copy in other_w:
         copy.start()
 
+    drains.extend(copy.wait_send for copy in other_w)
+
     lane = lax.broadcasted_iota(jnp.int32, (VB, 128), 1)
     for a in range(2):
         for xs in range(NX):
@@ -131,97 +142,77 @@
     def chunk(t, zz):
         return aq.at[zz] if t == 0 else (ak, av)[t - 1].at[half, zz]
 
-    def forward(zz):
-        for t in (1, 2):
-            pltpu.make_async_remote_copy(
-                src_ref=chunk(t, zz), dst_ref=chunk(t, zz), send_sem=s_f.at[t - 1, zz], recv_sem=r_f.at[t - 1, zz],
+    def forward(t, zz):
+        pltpu.make_async_remote_copy(
+            src_ref=chunk(t, zz), dst_ref=chunk(t, zz), send_sem=s_f.at[t - 1, zz], recv_sem=r_f.at[t - 1, zz],
+            device_id=core_peer, device_id_type=MESH,
+        ).start()
+
+    vf = []
+
+    def share_video():
+        for t, ref in enumerate((vk, vv)):
+            for xs in range(NX):
+                wait(ref.at[c, xs], r_pb.at[t, xs])
+            copy = pltpu.make_async_remote_copy(
+                src_ref=ref.at[c], dst_ref=ref.at[c], send_sem=s_vf.at[t], recv_sem=r_vf.at[t],
                 device_id=core_peer, device_id_type=MESH,
-            ).start()
-
-    forward(z)
-    sent = []
-    for k in range(1, NZ // 2 + 1):
-        hops = [(0, t) for t in range(3)] + [(1, t) for t in range(3)]
-        if k == NZ // 2:
-            hops = [(0, 0), (0, 1), (1, 2)]
-        for way, t in hops:
-            zz = (z - k + 1 + NZ) % NZ if way == 0 else (z + k - 1) % NZ
-            to = (z + 1) % NZ if way == 0 else (z + NZ - 1) % NZ
-            copy = pltpu.make_async_remote_copy(
-                src_ref=chunk(t, zz), dst_ref=chunk(t, zz), send_sem=s_z.at[way, t, k - 1], recv_sem=r_z.at[way, t, k - 1],
-                device_id=dev(yh, x, to, yl, c), device_id_type=MESH,
             )
             copy.start()
-            sent.append(copy)
-        for way, t in hops:
-            zz = (z - k + NZ) % NZ if way == 0 else (z + k) % NZ
-            wait(chunk(t, zz), r_z.at[way, t, k - 1])
-        if k < NZ // 2:
-            forward((z - k + NZ) % NZ)
-            forward((z + k) % NZ)
-        else:
-            forward((z + k) % NZ)
-
-    vf = []
-    for t, ref in enumerate((vk, vv)):
-        for xs in range(NX):
-            wait(ref.at[c, xs], r_pb.at[t, xs])
-        copy = pltpu.make_async_remote_copy(
-            src_ref=ref.at[c], dst_ref=ref.at[c], send_sem=s_vf.at[t], recv_sem=r_vf.at[t],
-            device_id=core_peer, device_id_type=MESH,
+            vf.append(copy)
+
+    def hop_copy(way, t, k):
+        zz = (z - k + 1 + NZ) % NZ if way == 0 else (z + k - 1) % NZ
+        to = (z + 1) % NZ if way == 0 else (z + NZ - 1) % NZ
+        return pltpu.make_async_remote_copy(
+            src_ref=chunk(t, zz), dst_ref=chunk(t, zz), send_sem=s_z.at[way, t, k - 1], recv_sem=r_z.at[way, t, k - 1],
+            device_id=dev(yh, x, to, yl, c), device_id_type=MESH,
         )
-        copy.start()
-        vf.append(copy)
-    for xs in range(NX):
-        wait(vq.at[xs], r_pb.at[2, xs])
-
-    def late(zz, carry):
-        wait(ak.at[other_half, zz], r_f.at[0, zz])
-        wait(av.at[other_half, zz], r_f.at[1, zz])
-        return carry
-
-    lax.fori_loop(0, NZ, late, 0)
-
-    ones_win = jnp.ones((WIN * AB, HD), BF16)
-
-    def video_block(n, carry):
-        xs, i = n // 2, n % 2
-        start = ws[((c * NX + xs) * NZ + z) * 2 + i]
-        blocks = pl.ds(start, WIN)
-        q = vq[xs, pl.ds(pl.multiple_of(i * VB, VB), VB), :]
-        s = nt(q, ak_flat[blocks].reshape(WIN * AB, HD))
-        top = jnp.max(s, axis=1, keepdims=True)
-        p = jnp.exp2((s - top) * C2).astype(BF16)
-        v = jnp.concatenate([av_flat[blocks].reshape(WIN * AB, HD), ones_win], axis=1)
-        o = jnp.dot(p, v, preferred_element_type=F32)
-        vo[xs, i] = (o[:, :HD] / o[:, HD:]).astype(BF16).reshape(2, VB // 2, HD)
-        return carry
-
-    lax.fori_loop(0, 2 * NX, video_block, 0)
-
-    my_slot = yh * NX + x
-
-    def vo_copy(j, k):
-        return pltpu.make_async_remote_copy(
-            src_ref=vo.at[(x + j) % NX, :, k], dst_ref=va.at[my_slot], send_sem=s_vo.at[j, k], recv_sem=r_vo.at[my_slot],
-            device_id=dev(c, (x + j) % NX, z, yl, k), device_id_type=MESH,
-        )
-
-    for j in range(NX):
-        for k in range(2):
-            copy = vo_copy(j, k)
-            if j:
-                copy.start()
-            else:
-                to_self = is_self & (c == k)
-
-                @pl.when(to_self)
-                def _(k=k):
-                    pltpu.make_async_copy(vo.at[x, :, k], va.at[my_slot], r_vo.at[my_slot]).start()
-
-                @pl.when(jnp.logical_not(to_self))
-                def _(copy=copy):
-                    copy.start()
+
+    def arrived(way, t, k):
+        zz = (z - k + NZ) % NZ if way == 0 else (z + k) % NZ
+        wait(chunk(t, zz), r_z.at[way, t, k - 1])
+        if t:
+            forward(t, zz)
+
+    sent = []
+    last_hops = [(0, 1), (1, 2), (0, 0)]
+
+    def hops(k):
+        return last_hops if k == NZ // 2 else [(way, t) for t in (1, 2, 0) for way in range(2)]
+
+    for k in range(1, NZ // 2 + 1):
+        if k == NZ // 2:
+            share_video()
+        for t in (1, 2, 0):
+            for way in range(2):
+                if k == 1:
+                    if t and way == 0:
+                        forward(t, z)
+                else:
+                    arrived(way, t, k - 1)
+                if (way, t) in hops(k):
+                    sent.append(hop_copy(way, t, k))
+                    sent[-1].start()
+
+    def gather_end():
+        for way, t in last_hops:
+            arrived(way, t, NZ // 2)
+
+    def gather_sent():
+        for copy in sent:
+            copy.wait_send()
+
+        def one(zz, carry):
+            wait(ak.at[half, zz], s_f.at[0, zz])
+            wait(av.at[half, zz], s_f.at[1, zz])
+            return carry
+
+        lax.fori_loop(0, NZ, one, 0)
+
+    drains.append(gather_sent)
+
+    drains.extend(copy.wait_send for copy in vf)
 
     for t, ref in enumerate((vk, vv)):
         wait(ref.at[1 - c], r_vf.at[t])
@@ -232,6 +223,7 @@
     ones_vid = jnp.ones((2 * NX * VR, HD), BF16)
 
     def audio_pair(it, carry):
+        pl.when(it == NZ // 4)(gather_end)
         z0, z1 = (z + 2 * it) % NZ, (z + 2 * it + 1) % NZ
         q = jnp.concatenate([aq[z0].reshape(NX * AR, HD), aq[z1].reshape(NX * AR, HD)], axis=0)
         zz = (z + 2 * it + u_of) % NZ
@@ -276,26 +268,88 @@
 
     lax.fori_loop(0, NZ // 2, audio_pair, 0)
 
+    def parts_sent():
+        for d in range(1, NZ):
+            wait(po.at[d], s_p.at[0, d])
+            wait(pst.at[d], s_p.at[1, d])
+
+    drains.append(parts_sent)
+    for xs in range(NX):
+        wait(vq.at[xs], r_pb.at[2, xs])
+
+    def late(zz, carry):
+        wait(ak.at[other_half, zz], r_f.at[0, zz])
+        wait(av.at[other_half, zz], r_f.at[1, zz])
+        return carry
+
+    lax.fori_loop(0, NZ, late, 0)
+
+    ones_win = jnp.ones((WIN * AB, HD), BF16)
+
+    my_slot = yh * NX + x
+
+    def video_rows(n, carry):
+        j = (n + 2) % NX
+        xs = (x + j) % NX
+        for i in range(2):
+            start = ws[((c * NX + xs) * NZ + z) * 2 + i]
+            blocks = pl.ds(start, WIN)
+            s = nt(vq[xs, pl.ds(i * VB, VB), :], ak_flat[blocks].reshape(WIN * AB, HD))
+            top = jnp.max(s, axis=1, keepdims=True)
+            p = jnp.exp2((s - top) * C2).astype(BF16)
+            v = jnp.concatenate([av_flat[blocks].reshape(WIN * AB, HD), ones_win], axis=1)
+            o = jnp.dot(p, v, preferred_element_type=F32)
+            o = (o[:, :HD] / o[:, HD:]).astype(BF16)
+            at = pl.ds(pl.multiple_of(jnp.where(yl == i, VB // 2, 0), VB // 2), VB // 2)
+            for k in range(2):
+                vo[xs, k, at, :] = o[k * VB // 2 : (k + 1) * VB // 2]
+        for k in range(2):
+            for m, (to, rows) in enumerate(((c, pl.ds(VB // 4, VB * 3 // 4)), (1 - c, pl.ds(0, VB // 4)))):
+                src, dst, recv = vo.at[xs, k, rows], va.at[my_slot, rows], r_vo.at[m, my_slot]
+                to_self = (j == 0) & (yh == to) & (c == k)
+
+                @pl.when(to_self)
+                def _(src=src, dst=dst, recv=recv):
+                    pltpu.make_async_copy(src, dst, recv).start()
+
+                @pl.when(jnp.logical_not(to_self))
+                def _(src=src, dst=dst, recv=recv, to=to, k=k, m=m):
+                    pltpu.make_async_remote_copy(
+                        src_ref=src, dst_ref=dst, send_sem=s_vo.at[m, j, k], recv_sem=recv,
+                        device_id=dev(to, xs, z, yl, k), device_id_type=MESH,
+                    ).start()
+
+        return carry
+
+    lax.fori_loop(0, NX, video_rows, 0)
+
+    def rows_sent(src, sems, to):
+        for j in range(NX):
+            for k in range(2):
+                if j:
+                    wait(src, sems.at[j, k])
+                else:
+                    pl.when(jnp.logical_not((yh == to) & (c == k)))(lambda k=k: wait(src, sems.at[0, k]))
+
+    drains.append(lambda: rows_sent(va.at[my_slot, pl.ds(VB // 4, VB * 3 // 4)], s_vo.at[0], c))
+    drains.append(lambda: rows_sent(va.at[my_slot, pl.ds(0, VB // 4)], s_vo.at[1], 1 - c))
+
     for copy in own_w:
         copy.wait()
     for t, ref in enumerate((wv, wa)):
         wait(ref.at[1 - c], r_w.at[t])
     for h in range(2 * NX):
-        wait(va.at[h], r_vo.at[h])
-    xv = jnp.concatenate(
-        [
-            jnp.concatenate([va[h, 1 - yl] for h in range(2 * NX)], axis=1),
-            jnp.concatenate([va[h, yl] for h in range(2 * NX)], axis=1),
-        ],
-        axis=0,
-    )
+        wait(va.at[h, pl.ds(VB // 4, VB * 3 // 4)], r_vo.at[0, h])
+        wait(va.at[h, pl.ds(0, VB // 4)], r_vo.at[1, h])
+    xv = jnp.concatenate([va[h] for h in range(2 * NX)], axis=1)
     n_chunks = ysend.shape[0]
     width = ysend.shape[2]
 
-    def y_copy(n):
+    def y_copy(n, m):
+        rows = pl.ds(m * VB // 4, VB // 4)
         return pltpu.make_async_remote_copy(
-            src_ref=ysend.at[n], dst_ref=yrecv.at[n], send_sem=s_y.at[n], recv_sem=r_y.at[n],
-            device_id=yl_peer, device_id_type=MESH,
+            src_ref=ysend.at[n, rows], dst_ref=yrecv.at[n, rows], send_sem=s_y.at[m, n], recv_sem=r_y.at[m, n],
+            device_id=(cross_peer, yl_peer)[m], device_id_type=MESH,
         )
 
     def project(n, carry):
@@ -304,10 +358,21 @@
         y = jnp.dot(xv, w, preferred_element_type=F32)
         ysend[n] = y[: VB // 2].astype(BF16)
         yown[n] = y[VB // 2 :]
-        y_copy(n).start()
+        for m in range(2):
+            y_copy(n, m).start()
         return carry
 
     lax.fori_loop(0, n_chunks, project, 0)
+
+    def y_sent():
+        def one(n, carry):
+            for m in range(2):
+                y_copy(n, m).wait_send()
+            return carry
+
+        lax.fori_loop(0, n_chunks, one, 0)
+
+    drains.append(y_sent)
 
     for d in range(1, NZ):
         wait(pr.at[d], r_p.at[0, d])
@@ -341,8 +406,11 @@
                 def _(copy=copy):
                     copy.start()
 
+    drains.append(lambda: rows_sent(aa.at[my_slot], s_ao, c))
+
     def finish(n, carry):
-        y_copy(n).wait_recv()
+        for m in range(2):
+            y_copy(n, m).wait_recv()
         at = pl.ds(pl.multiple_of(n * width, width), width)
         ov[:, at] = (yown[n] + yrecv[n].astype(F32)).astype(BF16)
         return carry
@@ -360,52 +428,12 @@
         src_ref=asend.at[1 - yl], dst_ref=arecv, send_sem=s_ya, recv_sem=r_ya, device_id=yl_peer, device_id_type=MESH
     )
     last.start()
+    drains.append(last.wait_send)
     last.wait_recv()
     oa[...] = (asend[yl] + arecv[...]).astype(BF16)
 
-    last.wait_send()
-    for copy in other_w + vf + sent:
-        copy.wait_send()
-
-    def y_sent(n, carry):
-        y_copy(n).wait_send()
-        return carry
-
-    lax.fori_loop(0, n_chunks, y_sent, 0)
-
-    def f_sent(zz, carry):
-        wait(ak.at[half, zz], s_f.at[0, zz])
-        wait(av.at[half, zz], s_f.at[1, zz])
-        return carry
-
-    lax.fori_loop(0, NZ, f_sent, 0)
-    for d in range(1, NZ):
-        wait(po.at[d], s_p.at[0, d])
-        wait(pst.at[d], s_p.at[1, d])
-
-    def sent_exchange(j):
-        for t in range(3):
-            wait(aq.at[z, x], s_pa.at[t, j])
-            wait(vq.at[x], s_pb.at[t, j])
-
-    for j in range(1, NX):
-        sent_exchange(j)
-
-    @pl.when(jnp.logical_not(is_self))
-    def _():
-        sent_exchange(0)
-
-    for j in range(NX):
-        for k in range(2):
-
-            def done(j=j, k=k):
-                wait(va.at[my_slot], s_vo.at[j, k])
-                wait(aa.at[my_slot], s_ao.at[j, k])
-
-            if j:
-                done()
-            else:
-                pl.when(jnp.logical_not(is_self & (c == k)))(done)
+    for drain in drains:
+        drain()
 
 
 def shards(vq, vk, vv, aq, ak, av, ws, wv, wa):
@@ -423,8 +451,8 @@
         vmem((2,) + wv.shape, BF16),
         vmem((2,) + wa.shape, BF16),
         vmem((2, NX, VR, HD), BF16),
-        vmem((NX, 2, 2, VB // 2, HD), BF16),
-        vmem((2 * NX, 2, VB // 2, HD), BF16),
+        vmem((NX, 2, VB, HD), BF16),
+        vmem((2 * NX, VB, HD), BF16),
         vmem((NZ, NX * AR, HD), BF16),
         vmem((NZ, 8, HD), F32),
         vmem((NZ, NX * AR, HD), BF16),
@@ -442,10 +470,10 @@
         dma((2, NZ)), dma((2, NZ)),
         dma((2,)), dma((2,)),
         dma((2,)), dma((2,)),
-        dma((NX, 2)), dma((2 * NX,)),
+        dma((2, NX, 2)), dma((2, 2 * NX)),
         dma((2, NZ)), dma((2, NZ)),
         dma((NX, 2)), dma((2 * NX,)),
-        dma((n_chunks,)), dma((n_chunks,)),
+        dma((2, n_chunks)), dma((2, n_chunks)),
         dma, dma,
         dma((2,)),
     ]
@@ -460,7 +488,7 @@
         out_specs=(pl.BlockSpec(memory_space=pltpu.VMEM), pl.BlockSpec(memory_space=pltpu.VMEM)),
         scratch_shapes=scratch,
         compiler_params=pltpu.CompilerParams(
-            collective_id=0, has_side_effects=True, vmem_limit_bytes=48 * 1024 * 1024
+            collective_id=0, has_side_effects=True, vmem_limit_bytes=60 * 1024 * 1024
         ),
         cost_estimate=pl.CostEstimate(flops=3_000_000_000, bytes_accessed=16_000_000, transcendentals=4_000_000),
     )(ws, vq, vk, vv, aq, ak, av, wv, wa)

time: 76.7 us -> 63.7 us (0.83)
  Pallas kernels: 66.9 us -> 59.5 us
  local copies, waits for them, and re-layouts: 8.77 us -> 3.24 us
    pallas_call x1, Pallas kernels: 66.9 us -> 59.5 us  [shards(): pl.pallas_call(kernel, out_shape=(jax.ShapeDtypeStruct((vq.shape[0] // 4,...]
    unnamed x18 -> x2, local copies, waits for them, and re-layouts: 8.77 us -> 3.24 us
where the time goes in v2:
time: 63.7 us; the launch traced here: 63.4 us
  Pallas kernels  59.5 us (93%)
  local copies, waits for them, and re-layouts  3.24 us (5%)
  between operations  0.64 us (1%)
    pallas_call x1, Pallas kernels, shards(): pl.pallas_call(kernel, out_shape=(jax.ShapeDtypeStruct((vq.shape[0] // 4,...  59.5 us
    unnamed x2, local copies, waits for them, and re-layouts  3.24 us

profile of v2, /device:TPU:1, one launch (start us, length us, event | category | flops | bytes accessed | tf_op | source)
XLA Modules:
  0.0 63.4 jit_solution(4486005727969226808)
XLA Ops:
  0.6 59.5 %shard_map.104 = (bf16[64,4096]{1,0:T(8,128)(2,1)}, bf16[8,2048]{1,0:T(8,128)(2,1)}) custom-call(s32[128]{0:T(128)} %ws.1, bf16[256,512]{1,0:T(8,128)(2,1)} %vq_in.1, bf16[256,512]{1,0:T(8,128)(2,1)} %vk_in.1, bf16[256,512]{1,0:T(8,128)(2,1)} %vv_in.1, bf16[32,512]{1,0:T(8,128)(2,1)} %aq_in.1, bf16[32,512]{1,0:T(8,128)(2,1)} %ak_in.1, ...), custom_call_target="tpu_custom_call" | custom-call | flops 3000000000 | bytes 16000000 | tf_op jit(solution)/shard_map/pallas_call | solution.py:481
  60.2 1.9 %copy.13 = bf16[64,4096]{1,0:T(8,128)(2,1)} copy(bf16[64,4096]{1,0:T(8,128)(2,1)} %get-tuple-element.4) | data formatting | bytes 1048576
  62.1 1.4 %copy.14 = bf16[8,2048]{1,0:T(8,128)(2,1)} copy(bf16[8,2048]{1,0:T(8,128)(2,1)} %get-tuple-element.5) | data formatting | bytes 65536

commit v3 on v2

--- a/solution.py
+++ b/solution.py
@@ -95,6 +95,13 @@
         exchange(aq_in.at[:, cols(j)], aq.at[z, x], s_pa.at[0, j], r_pa.at[0, x], j)
         exchange(ak_in.at[:, cols(j)], ak.at[here, z], s_pa.at[1, j], r_pa.at[1, x], j)
         exchange(av_in.at[:, cols(j)], av.at[here, z], s_pa.at[2, j], r_pa.at[2, x], j)
+    def audio_sent(j):
+        for t in range(3):
+            wait(aq.at[z, x], s_pa.at[t, j])
+
+    for j in range(1, NX):
+        audio_sent(j)
+    pl.when(jnp.logical_not(is_self))(lambda: audio_sent(0))
     for t, (src, dst) in enumerate(((vk_in, vk.at[yh]), (vv_in, vv.at[yh]), (vq_in, vq))):
         for j in range(NX):
             exchange(src.at[:, cols(j)], dst.at[x], s_pb.at[t, j], r_pb.at[t, x], j)
@@ -102,7 +109,6 @@
     def exchange_sent():
         def one(j):
             for t in range(3):
-                wait(aq.at[z, x], s_pa.at[t, j])
                 wait(vq.at[x], s_pb.at[t, j])
 
         for j in range(1, NX):
@@ -110,18 +116,6 @@
         pl.when(jnp.logical_not(is_self))(lambda: one(0))
 
     drains.append(exchange_sent)
-
-    other_w = [
-        pltpu.make_async_remote_copy(
-            src_ref=src, dst_ref=dst.at[c], send_sem=s_w.at[t], recv_sem=r_w.at[t],
-            device_id=core_peer, device_id_type=MESH,
-        )
-        for t, (src, dst) in enumerate(((wv_in, wv), (wa_in, wa)))
-    ]
-    for copy in other_w:
-        copy.start()
-
-    drains.extend(copy.wait_send for copy in other_w)
 
     lane = lax.broadcasted_iota(jnp.int32, (VB, 128), 1)
     for a in range(2):
@@ -175,33 +169,33 @@
         if t:
             forward(t, zz)
 
-    sent = []
     last_hops = [(0, 1), (1, 2), (0, 0)]
 
     def hops(k):
         return last_hops if k == NZ // 2 else [(way, t) for t in (1, 2, 0) for way in range(2)]
 
-    for k in range(1, NZ // 2 + 1):
-        if k == NZ // 2:
-            share_video()
+    def hop(k):
         for t in (1, 2, 0):
             for way in range(2):
-                if k == 1:
-                    if t and way == 0:
-                        forward(t, z)
-                else:
+                if k > 1:
                     arrived(way, t, k - 1)
+                elif t and way == 0:
+                    forward(t, z)
                 if (way, t) in hops(k):
-                    sent.append(hop_copy(way, t, k))
-                    sent[-1].start()
+                    hop_copy(way, t, k).start()
+
+    for k in range(1, NZ // 2):
+        hop(k)
+    share_video()
 
     def gather_end():
         for way, t in last_hops:
             arrived(way, t, NZ // 2)
 
     def gather_sent():
-        for copy in sent:
-            copy.wait_send()
+        for k in range(1, NZ // 2 + 1):
+            for way, t in hops(k):
+                hop_copy(way, t, k).wait_send()
 
         def one(zz, carry):
             wait(ak.at[half, zz], s_f.at[0, zz])
@@ -213,6 +207,18 @@
     drains.append(gather_sent)
 
     drains.extend(copy.wait_send for copy in vf)
+
+    other_w = [
+        pltpu.make_async_remote_copy(
+            src_ref=src, dst_ref=dst.at[c], send_sem=s_w.at[t], recv_sem=r_w.at[t],
+            device_id=core_peer, device_id_type=MESH,
+        )
+        for t, (src, dst) in enumerate(((wv_in, wv), (wa_in, wa)))
+    ]
+    for copy in other_w:
+        copy.start()
+
+    drains.extend(copy.wait_send for copy in other_w)
 
     for t, ref in enumerate((vk, vv)):
         wait(ref.at[1 - c], r_vf.at[t])
@@ -222,11 +228,14 @@
     eye = lax.broadcasted_iota(jnp.int32, (HD, HD), 0) == lax.broadcasted_iota(jnp.int32, (HD, HD), 1)
     ones_vid = jnp.ones((2 * NX * VR, HD), BF16)
 
-    def audio_pair(it, carry):
-        pl.when(it == NZ // 4)(gather_end)
-        z0, z1 = (z + 2 * it) % NZ, (z + 2 * it + 1) % NZ
+    def audio_pair(n, carry):
+        pl.when(n == 1)(lambda: hop(NZ // 2))
+        pl.when(n == NZ // 2 - 1)(gather_end)
+        d0 = (n + 1) % (NZ // 2)
+        d1 = jnp.where(d0 == 0, NZ // 2, NZ - d0)
+        z0, z1 = (z + d0) % NZ, (z + d1) % NZ
         q = jnp.concatenate([aq[z0].reshape(NX * AR, HD), aq[z1].reshape(NX * AR, HD)], axis=0)
-        zz = (z + 2 * it + u_of) % NZ
+        zz = jnp.where(u_of == 0, z0, z1)
         block = ((c * NX + x_of) * NZ + zz) * 2 + b_of
         q = jnp.concatenate([q, jnp.where(lane2 == block, 1.0, 0.0).astype(BF16)], axis=1)
         key = jnp.concatenate([vk[...].reshape(2 * NX * VR, HD), kb[...].reshape(2 * NX * VR, HD)], axis=1)
@@ -238,7 +247,7 @@
         part = (o[:, :HD] / o[:, HD:]).astype(BF16)
         level = top * C2 + jnp.log2(o[:, HD:])
         for u in range(2):
-            d = 2 * it + u
+            d = d1 if u else d0
             rows = slice(u * NX * AR, (u + 1) * NX * AR)
             flat = jnp.sum(jnp.where(eye, level[rows], 0.0), axis=0, keepdims=True)
             flat = jnp.broadcast_to(flat, (8, HD))
@@ -258,12 +267,12 @@
                 keep()
             else:
 
-                @pl.when(it == 0)
+                @pl.when(d == 0)
                 def _(rows=rows, flat=flat):
                     pr[0] = part[rows]
                     prs[0] = flat
 
-                pl.when(it > 0)(keep)
+                pl.when(d > 0)(keep)
         return carry
 
     lax.fori_loop(0, NZ // 2, audio_pair, 0)
@@ -333,46 +342,6 @@
 
     drains.append(lambda: rows_sent(va.at[my_slot, pl.ds(VB // 4, VB * 3 // 4)], s_vo.at[0], c))
     drains.append(lambda: rows_sent(va.at[my_slot, pl.ds(0, VB // 4)], s_vo.at[1], 1 - c))
-
-    for copy in own_w:
-        copy.wait()
-    for t, ref in enumerate((wv, wa)):
-        wait(ref.at[1 - c], r_w.at[t])
-    for h in range(2 * NX):
-        wait(va.at[h, pl.ds(VB // 4, VB * 3 // 4)], r_vo.at[0, h])
-        wait(va.at[h, pl.ds(0, VB // 4)], r_vo.at[1, h])
-    xv = jnp.concatenate([va[h] for h in range(2 * NX)], axis=1)
-    n_chunks = ysend.shape[0]
-    width = ysend.shape[2]
-
-    def y_copy(n, m):
-        rows = pl.ds(m * VB // 4, VB // 4)
-        return pltpu.make_async_remote_copy(
-            src_ref=ysend.at[n, rows], dst_ref=yrecv.at[n, rows], send_sem=s_y.at[m, n], recv_sem=r_y.at[m, n],
-            device_id=(cross_peer, yl_peer)[m], device_id_type=MESH,
-        )
-
-    def project(n, carry):
-        at = pl.ds(pl.multiple_of(n * width, width), width)
-        w = jnp.concatenate([wv[0, :, at], wv[1, :, at]], axis=0)
-        y = jnp.dot(xv, w, preferred_element_type=F32)
-        ysend[n] = y[: VB // 2].astype(BF16)
-        yown[n] = y[VB // 2 :]
-        for m in range(2):
-            y_copy(n, m).start()
-        return carry
-
-    lax.fori_loop(0, n_chunks, project, 0)
-
-    def y_sent():
-        def one(n, carry):
-            for m in range(2):
-                y_copy(n, m).wait_send()
-            return carry
-
-        lax.fori_loop(0, n_chunks, one, 0)
-
-    drains.append(y_sent)
 
     for d in range(1, NZ):
         wait(pr.at[d], r_p.at[0, d])
@@ -408,14 +377,45 @@
 
     drains.append(lambda: rows_sent(aa.at[my_slot], s_ao, c))
 
-    def finish(n, carry):
+    for copy in own_w:
+        copy.wait()
+    for t, ref in enumerate((wv, wa)):
+        wait(ref.at[1 - c], r_w.at[t])
+    for h in range(2 * NX):
+        wait(va.at[h, pl.ds(VB // 4, VB * 3 // 4)], r_vo.at[0, h])
+        wait(va.at[h, pl.ds(0, VB // 4)], r_vo.at[1, h])
+    xv = jnp.concatenate([va[h] for h in range(2 * NX)], axis=1)
+    n_chunks = ysend.shape[0]
+    width = ysend.shape[2]
+
+    def y_copy(n, m):
+        rows = pl.ds(m * VB // 4, VB // 4)
+        return pltpu.make_async_remote_copy(
+            src_ref=ysend.at[n, rows], dst_ref=yrecv.at[n, rows], send_sem=s_y.at[m, n], recv_sem=r_y.at[m, n],
+            device_id=(cross_peer, yl_peer)[m], device_id_type=MESH,
+        )
+
+    def project(n, carry):
+        at = pl.ds(pl.multiple_of(n * width, width), width)
+        w = jnp.concatenate([wv[0, :, at], wv[1, :, at]], axis=0)
+        y = jnp.dot(xv, w, preferred_element_type=F32)
+        ysend[n] = y[: VB // 2].astype(BF16)
+        yown[n] = y[VB // 2 :]
         for m in range(2):
-            y_copy(n, m).wait_recv()
-        at = pl.ds(pl.multiple_of(n * width, width), width)
-        ov[:, at] = (yown[n] + yrecv[n].astype(F32)).astype(BF16)
+            y_copy(n, m).start()
         return carry
 
-    lax.fori_loop(0, n_chunks, finish, 0)
+    lax.fori_loop(0, n_chunks, project, 0)
+
+    def y_sent():
+        def one(n, carry):
+            for m in range(2):
+                y_copy(n, m).wait_send()
+            return carry
+
+        lax.fori_loop(0, n_chunks, one, 0)
+
+    drains.append(y_sent)
 
     for h in range(2 * NX):
         wait(aa.at[h], r_ao.at[h])
@@ -429,11 +429,26 @@
     )
     last.start()
     drains.append(last.wait_send)
+
+    def finish(n, carry):
+        for m in range(2):
+            y_copy(n, m).wait_recv()
+        at = pl.ds(pl.multiple_of(n * width, width), width)
+        ov[:, at] = (yown[n] + yrecv[n].astype(F32)).astype(BF16)
+        return carry
+
+    lax.fori_loop(0, n_chunks, finish, 0)
+
     last.wait_recv()
     oa[...] = (asend[yl] + arecv[...]).astype(BF16)
 
     for drain in drains:
         drain()
+
+
+def hand_over(ov, oa, to_v, to_a):
+    to_v[...] = ov[...]
+    to_a[...] = oa[...]
 
 
 def shards(vq, vk, vv, aq, ak, av, ws, wv, wa):
@@ -478,7 +493,7 @@
         dma((2,)),
     ]
     any_spec = pl.BlockSpec(memory_space=pl.ANY)
-    return pl.pallas_call(
+    outs = pl.pallas_call(
         kernel,
         out_shape=(
             jax.ShapeDtypeStruct((vq.shape[0] // 4, dv), BF16),
@@ -492,6 +507,9 @@
         ),
         cost_estimate=pl.CostEstimate(flops=3_000_000_000, bytes_accessed=16_000_000, transcendentals=4_000_000),
     )(ws, vq, vk, vv, aq, ak, av, wv, wa)
+    return pl.pallas_call(
+        hand_over, out_shape=tuple(jax.ShapeDtypeStruct(o.shape, o.dtype) for o in outs)
+    )(*outs)
 
 
 def solution(mesh):

time: 63.7 us -> 58.3 us (0.915)
  local copies, waits for them, and re-layouts: 3.24 us -> 0 us
  Pallas kernels: 59.5 us -> 57.6 us
    pallas_call x1, Pallas kernels: 59.5 us -> 55.7 us  [shards(): pl.pallas_call(kernel, out_shape=(jax.ShapeDtypeStruct((vq.shape[0] // 4,...]
    unnamed x2 -> x0, local copies, waits for them, and re-layouts: 3.24 us -> none
    pallas_call x0 -> x1, Pallas kernels: none -> 1.87 us  [shards(): pl.pallas_call(hand_over, out_shape=tuple((jax.ShapeDtypeStruct(o.shape,...]
where the time goes in v3:
time: 58.3 us; the launch traced here: 58.2 us
  Pallas kernels  57.6 us (99%)
  between operations  0.64 us (1%)
    pallas_call x1, Pallas kernels, shards(): pl.pallas_call(kernel, out_shape=(jax.ShapeDtypeStruct((vq.shape[0] // 4,...  55.7 us
    pallas_call x1, Pallas kernels, shards(): pl.pallas_call(hand_over, out_shape=tuple((jax.ShapeDtypeStruct(o.shape,...  1.87 us

profile of v3, /device:TPU:1, one launch (start us, length us, event | category | flops | bytes accessed | tf_op | source)
XLA Modules:
  0.0 58.2 jit_solution(5762566377442370505)
XLA Ops:
  0.6 55.7 %shard_map.104 = (bf16[64,4096]{1,0:T(8,128)(2,1)}, bf16[8,2048]{1,0:T(8,128)(2,1)}) custom-call(s32[128]{0:T(128)} %ws.1, bf16[256,512]{1,0:T(8,128)(2,1)} %vq_in.1, bf16[256,512]{1,0:T(8,128)(2,1)} %vk_in.1, bf16[256,512]{1,0:T(8,128)(2,1)} %vv_in.1, bf16[32,512]{1,0:T(8,128)(2,1)} %aq_in.1, bf16[32,512]{1,0:T(8,128)(2,1)} %ak_in.1, ...), custom_call_target="tpu_custom_call" | custom-call | flops 3000000000 | bytes 16000000 | tf_op jit(solution)/shard_map/pallas_call | solution.py:496
  56.4 1.9 %shard_map.105 = (bf16[64,4096]{1,0:T(8,128)(2,1)}, bf16[8,2048]{1,0:T(8,128)(2,1)}) custom-call(bf16[64,4096]{1,0:T(8,128)(2,1)} %get-tuple-element.4.ov, bf16[8,2048]{1,0:T(8,128)(2,1)} %get-tuple-element.5.oa), custom_call_target="tpu_custom_call" | custom-call | tf_op jit(solution)/shard_map/pallas_call | solution.py:510

commit v4 on v3

--- a/solution.py
+++ b/solution.py
@@ -71,6 +71,18 @@
     greet(cross_peer)
     pl.semaphore_wait(barrier, len(group) + NZ + 1)
 
+    other_w = [
+        pltpu.make_async_remote_copy(
+            src_ref=src, dst_ref=dst.at[c], send_sem=s_w.at[t], recv_sem=r_w.at[t],
+            device_id=core_peer, device_id_type=MESH,
+        )
+        for t, (src, dst) in enumerate(((wv_in, wv), (wa_in, wa)))
+    ]
+    for copy in other_w:
+        copy.start()
+
+    drains.extend(copy.wait_send for copy in other_w)
+
     def exchange(src, dst, send, recv, j):
         remote = pltpu.make_async_remote_copy(
             src_ref=src, dst_ref=dst, send_sem=send, recv_sem=recv, device_id=peer(j), device_id_type=MESH
@@ -207,18 +219,6 @@
     drains.append(gather_sent)
 
     drains.extend(copy.wait_send for copy in vf)
-
-    other_w = [
-        pltpu.make_async_remote_copy(
-            src_ref=src, dst_ref=dst.at[c], send_sem=s_w.at[t], recv_sem=r_w.at[t],
-            device_id=core_peer, device_id_type=MESH,
-        )
-        for t, (src, dst) in enumerate(((wv_in, wv), (wa_in, wa)))
-    ]
-    for copy in other_w:
-        copy.start()
-
-    drains.extend(copy.wait_send for copy in other_w)
 
     for t, ref in enumerate((vk, vv)):
         wait(ref.at[1 - c], r_vf.at[t])
@@ -297,40 +297,54 @@
 
     my_slot = yh * NX + x
 
+    def send_rows(xs, j, k, m, to, rows):
+        src, dst, recv = vo.at[xs, k, rows], va.at[my_slot, rows], r_vo.at[m, my_slot]
+        to_self = (j == 0) & (yh == to) & (c == k)
+
+        @pl.when(to_self)
+        def _():
+            pltpu.make_async_copy(src, dst, recv).start()
+
+        @pl.when(jnp.logical_not(to_self))
+        def _():
+            pltpu.make_async_remote_copy(
+                src_ref=src, dst_ref=dst, send_sem=s_vo.at[m, j, k], recv_sem=recv,
+                device_id=dev(to, xs, z, yl, k), device_id_type=MESH,
+            ).start()
+
+    parts = ((1 - c, pl.ds(0, VB // 4)), (c, pl.ds(VB // 4, VB // 4)), (c, pl.ds(VB // 2, VB // 2)))
+
     def video_rows(n, carry):
         j = (n + 2) % NX
         xs = (x + j) % NX
-        for i in range(2):
-            start = ws[((c * NX + xs) * NZ + z) * 2 + i]
-            blocks = pl.ds(start, WIN)
-            s = nt(vq[xs, pl.ds(i * VB, VB), :], ak_flat[blocks].reshape(WIN * AB, HD))
-            top = jnp.max(s, axis=1, keepdims=True)
-            p = jnp.exp2((s - top) * C2).astype(BF16)
-            v = jnp.concatenate([av_flat[blocks].reshape(WIN * AB, HD), ones_win], axis=1)
-            o = jnp.dot(p, v, preferred_element_type=F32)
-            o = (o[:, :HD] / o[:, HD:]).astype(BF16)
-            at = pl.ds(pl.multiple_of(jnp.where(yl == i, VB // 2, 0), VB // 2), VB // 2)
+        own = n // NX
+        i = jnp.where(own == 1, yl, 1 - yl)
+        start = ws[((c * NX + xs) * NZ + z) * 2 + i]
+        blocks = pl.ds(start, WIN)
+        s = nt(vq[xs, pl.ds(pl.multiple_of(i * VB, VB), VB), :], ak_flat[blocks].reshape(WIN * AB, HD))
+        top = jnp.max(s, axis=1, keepdims=True)
+        p = jnp.exp2((s - top) * C2).astype(BF16)
+        v = jnp.concatenate([av_flat[blocks].reshape(WIN * AB, HD), ones_win], axis=1)
+        o = jnp.dot(p, v, preferred_element_type=F32)
+        o = (o[:, :HD] / o[:, HD:]).astype(BF16)
+        at = pl.ds(pl.multiple_of(own * (VB // 2), VB // 2), VB // 2)
+        for k in range(2):
+            vo[xs, k, at, :] = o[k * VB // 2 : (k + 1) * VB // 2]
+
+        @pl.when(own == 0)
+        def _():
             for k in range(2):
-                vo[xs, k, at, :] = o[k * VB // 2 : (k + 1) * VB // 2]
-        for k in range(2):
-            for m, (to, rows) in enumerate(((c, pl.ds(VB // 4, VB * 3 // 4)), (1 - c, pl.ds(0, VB // 4)))):
-                src, dst, recv = vo.at[xs, k, rows], va.at[my_slot, rows], r_vo.at[m, my_slot]
-                to_self = (j == 0) & (yh == to) & (c == k)
-
-                @pl.when(to_self)
-                def _(src=src, dst=dst, recv=recv):
-                    pltpu.make_async_copy(src, dst, recv).start()
-
-                @pl.when(jnp.logical_not(to_self))
-                def _(src=src, dst=dst, recv=recv, to=to, k=k, m=m):
-                    pltpu.make_async_remote_copy(
-                        src_ref=src, dst_ref=dst, send_sem=s_vo.at[m, j, k], recv_sem=recv,
-                        device_id=dev(to, xs, z, yl, k), device_id_type=MESH,
-                    ).start()
+                for m in range(2):
+                    send_rows(xs, j, k, m, *parts[m])
+
+        @pl.when(own == 1)
+        def _():
+            for k in range(2):
+                send_rows(xs, j, k, 2, *parts[2])
 
         return carry
 
-    lax.fori_loop(0, NX, video_rows, 0)
+    lax.fori_loop(0, 2 * NX, video_rows, 0)
 
     def rows_sent(src, sems, to):
         for j in range(NX):
@@ -340,8 +354,8 @@
                 else:
                     pl.when(jnp.logical_not((yh == to) & (c == k)))(lambda k=k: wait(src, sems.at[0, k]))
 
-    drains.append(lambda: rows_sent(va.at[my_slot, pl.ds(VB // 4, VB * 3 // 4)], s_vo.at[0], c))
-    drains.append(lambda: rows_sent(va.at[my_slot, pl.ds(0, VB // 4)], s_vo.at[1], 1 - c))
+    for m, (to, rows) in enumerate(parts):
+        drains.append(lambda m=m, to=to, rows=rows: rows_sent(va.at[my_slot, rows], s_vo.at[m], to))
 
     for d in range(1, NZ):
         wait(pr.at[d], r_p.at[0, d])
@@ -381,10 +395,14 @@
         copy.wait()
     for t, ref in enumerate((wv, wa)):
         wait(ref.at[1 - c], r_w.at[t])
-    for h in range(2 * NX):
-        wait(va.at[h, pl.ds(VB // 4, VB * 3 // 4)], r_vo.at[0, h])
-        wait(va.at[h, pl.ds(0, VB // 4)], r_vo.at[1, h])
-    xv = jnp.concatenate([va[h] for h in range(2 * NX)], axis=1)
+
+    def rows_here(*which):
+        for h in range(2 * NX):
+            for m in which:
+                wait(va.at[h, parts[m][1]], r_vo.at[m, h])
+        at = slice(0, VB // 2) if 0 in which else slice(VB // 2, VB)
+        return jnp.concatenate([va[h, at, :] for h in range(2 * NX)], axis=1)
+
     n_chunks = ysend.shape[0]
     width = ysend.shape[2]
 
@@ -395,17 +413,28 @@
             device_id=(cross_peer, yl_peer)[m], device_id_type=MESH,
         )
 
-    def project(n, carry):
+    def project(x_rows, n):
         at = pl.ds(pl.multiple_of(n * width, width), width)
         w = jnp.concatenate([wv[0, :, at], wv[1, :, at]], axis=0)
-        y = jnp.dot(xv, w, preferred_element_type=F32)
-        ysend[n] = y[: VB // 2].astype(BF16)
-        yown[n] = y[VB // 2 :]
+        return jnp.dot(x_rows, w, preferred_element_type=F32)
+
+    x_other = rows_here(0, 1)
+
+    def project_other(n, carry):
+        ysend[n] = project(x_other, n).astype(BF16)
         for m in range(2):
             y_copy(n, m).start()
         return carry
 
-    lax.fori_loop(0, n_chunks, project, 0)
+    lax.fori_loop(0, n_chunks, project_other, 0)
+
+    x_own = rows_here(2)
+
+    def project_own(n, carry):
+        yown[n] = project(x_own, n)
+        return carry
+
+    lax.fori_loop(0, n_chunks, project_own, 0)
 
     def y_sent():
         def one(n, carry):
@@ -415,7 +444,6 @@
 
         lax.fori_loop(0, n_chunks, one, 0)
 
-    drains.append(y_sent)
 
     for h in range(2 * NX):
         wait(aa.at[h], r_ao.at[h])
@@ -428,7 +456,9 @@
         src_ref=asend.at[1 - yl], dst_ref=arecv, send_sem=s_ya, recv_sem=r_ya, device_id=yl_peer, device_id_type=MESH
     )
     last.start()
-    drains.append(last.wait_send)
+
+    for drain in drains:
+        drain()
 
     def finish(n, carry):
         for m in range(2):
@@ -442,8 +472,8 @@
     last.wait_recv()
     oa[...] = (asend[yl] + arecv[...]).astype(BF16)
 
-    for drain in drains:
-        drain()
+    last.wait_send()
+    y_sent()
 
 
 def hand_over(ov, oa, to_v, to_a):
@@ -485,7 +515,7 @@
         dma((2, NZ)), dma((2, NZ)),
         dma((2,)), dma((2,)),
         dma((2,)), dma((2,)),
-        dma((2, NX, 2)), dma((2, 2 * NX)),
+        dma((3, NX, 2)), dma((3, 2 * NX)),
         dma((2, NZ)), dma((2, NZ)),
         dma((NX, 2)), dma((2 * NX,)),
         dma((2, n_chunks)), dma((2, n_chunks)),

time: 58.3 us -> 56.1 us (0.962)
  Pallas kernels: 57.6 us -> 55.4 us
    pallas_call x1, Pallas kernels: 55.7 us -> 53.5 us  [shards(): pl.pallas_call(kernel, out_shape=(jax.ShapeDtypeStruct((vq.shape[0] // 4,...]
where the time goes in v4:
time: 56.1 us; the launch traced here: 56 us
  Pallas kernels  55.4 us (99%)
  between operations  0.64 us (1%)
    pallas_call x1, Pallas kernels, shards(): pl.pallas_call(kernel, out_shape=(jax.ShapeDtypeStruct((vq.shape[0] // 4,...  53.5 us
    pallas_call x1, Pallas kernels, shards(): pl.pallas_call(hand_over, out_shape=tuple((jax.ShapeDtypeStruct(o.shape,...  1.87 us

profile of v4, /device:TPU:1, one launch (start us, length us, event | category | flops | bytes accessed | tf_op | source)
XLA Modules:
  0.0 56.0 jit_solution(13540995225914179078)
XLA Ops:
  0.6 53.5 %shard_map.104 = (bf16[64,4096]{1,0:T(8,128)(2,1)}, bf16[8,2048]{1,0:T(8,128)(2,1)}) custom-call(s32[128]{0:T(128)} %ws.1, bf16[256,512]{1,0:T(8,128)(2,1)} %vq_in.1, bf16[256,512]{1,0:T(8,128)(2,1)} %vk_in.1, bf16[256,512]{1,0:T(8,128)(2,1)} %vv_in.1, bf16[32,512]{1,0:T(8,128)(2,1)} %aq_in.1, bf16[32,512]{1,0:T(8,128)(2,1)} %ak_in.1, ...), custom_call_target="tpu_custom_call" | custom-call | flops 3000000000 | bytes 16000000 | tf_op jit(solution)/shard_map/pallas_call | solution.py:526
  54.1 1.9 %shard_map.105 = (bf16[64,4096]{1,0:T(8,128)(2,1)}, bf16[8,2048]{1,0:T(8,128)(2,1)}) custom-call(bf16[64,4096]{1,0:T(8,128)(2,1)} %get-tuple-element.4.ov, bf16[8,2048]{1,0:T(8,128)(2,1)} %get-tuple-element.5.oa), custom_call_target="tpu_custom_call" | custom-call | tf_op jit(solution)/shard_map/pallas_call | solution.py:540

commit v5 on v4

--- a/solution.py
+++ b/solution.py
@@ -30,7 +30,7 @@
 
 def kernel(
     ws, vq_in, vk_in, vv_in, aq_in, ak_in, av_in, wv_in, wa_in, ov, oa,
-    vq, vk, vv, aq, ak_flat, av_flat, wv, wa, kb, vo, va, po, pst, pr, prs, ao, aa, ysend, yrecv, yown, asend, arecv,
+    vq, vk, vv, aq, ak_flat, av_flat, wv, wa, kb, vo, va, po, pst, pr, prs, ao, aa, ysend, yrecv, yown, aown, asend, arecv,
     s_pa, r_pa, s_pb, r_pb, s_z, r_z, s_f, r_f, s_vf, r_vf, s_w, r_w, s_vo, r_vo, s_p, r_p, s_ao, r_ao, s_y, r_y, s_ya, r_ya, l_w,
 ):
     seq, head = lax.axis_index("seq"), lax.axis_index("head")
@@ -346,17 +346,6 @@
 
     lax.fori_loop(0, 2 * NX, video_rows, 0)
 
-    def rows_sent(src, sems, to):
-        for j in range(NX):
-            for k in range(2):
-                if j:
-                    wait(src, sems.at[j, k])
-                else:
-                    pl.when(jnp.logical_not((yh == to) & (c == k)))(lambda k=k: wait(src, sems.at[0, k]))
-
-    for m, (to, rows) in enumerate(parts):
-        drains.append(lambda m=m, to=to, rows=rows: rows_sent(va.at[my_slot, rows], s_vo.at[m], to))
-
     for d in range(1, NZ):
         wait(pr.at[d], r_p.at[0, d])
         wait(prs.at[d], r_p.at[1, d])
@@ -391,6 +380,17 @@
 
     drains.append(lambda: rows_sent(aa.at[my_slot], s_ao, c))
 
+    def rows_sent(src, sems, to):
+        for j in range(NX):
+            for k in range(2):
+                if j:
+                    wait(src, sems.at[j, k])
+                else:
+                    pl.when(jnp.logical_not((yh == to) & (c == k)))(lambda k=k: wait(src, sems.at[0, k]))
+
+    for m, (to, rows) in enumerate(parts):
+        drains.append(lambda m=m, to=to, rows=rows: rows_sent(va.at[my_slot, rows], s_vo.at[m], to))
+
     for copy in own_w:
         copy.wait()
     for t, ref in enumerate((wv, wa)):
@@ -428,34 +428,38 @@
 
     lax.fori_loop(0, n_chunks, project_other, 0)
 
-    x_own = rows_here(2)
-
-    def project_own(n, carry):
-        yown[n] = project(x_own, n)
-        return carry
-
-    lax.fori_loop(0, n_chunks, project_own, 0)
-
-    def y_sent():
-        def one(n, carry):
-            for m in range(2):
-                y_copy(n, m).wait_send()
-            return carry
-
-        lax.fori_loop(0, n_chunks, one, 0)
-
-
     for h in range(2 * NX):
         wait(aa.at[h], r_ao.at[h])
     xa = jnp.concatenate([aa[h] for h in range(2 * NX)], axis=1)
     for n in range(wa.shape[2] // 512):
         at = slice(n * 512, (n + 1) * 512)
         w = jnp.concatenate([wa[0, :, at], wa[1, :, at]], axis=0)
-        asend[:, :, at] = jnp.dot(xa, w, preferred_element_type=F32).reshape(2, 8, 512)
+        y = jnp.dot(xa, w, preferred_element_type=F32).reshape(2, 8, 512)
+        aown[:, :, at] = y
+        side = n * 1024 // wa.shape[2]
+        at = slice(n * 512 - side * wa.shape[2] // 2, (n + 1) * 512 - side * wa.shape[2] // 2)
+        asend[:, 8 * side : 8 * side + 8, at] = y.astype(BF16)
     last = pltpu.make_async_remote_copy(
         src_ref=asend.at[1 - yl], dst_ref=arecv, send_sem=s_ya, recv_sem=r_ya, device_id=yl_peer, device_id_type=MESH
     )
     last.start()
+
+    x_own = rows_here(2)
+
+    def project_own(n, carry):
+        yown[n] = project(x_own, n)
+        return carry
+
+    lax.fori_loop(0, n_chunks, project_own, 0)
+
+    def y_sent():
+        def one(n, carry):
+            for m in range(2):
+                y_copy(n, m).wait_send()
+            return carry
+
+        lax.fori_loop(0, n_chunks, one, 0)
+
 
     for drain in drains:
         drain()
@@ -470,7 +474,8 @@
     lax.fori_loop(0, n_chunks, finish, 0)
 
     last.wait_recv()
-    oa[...] = (asend[yl] + arecv[...]).astype(BF16)
+    theirs = arecv[...].astype(F32)
+    oa[...] = (aown[yl] + jnp.concatenate([theirs[:8], theirs[8:]], axis=1)).astype(BF16)
 
     last.wait_send()
     y_sent()
@@ -508,7 +513,8 @@
         vmem((n_chunks, VB // 2, dv // n_chunks), BF16),
         vmem((n_chunks, VB // 2, dv // n_chunks), F32),
         vmem((2, 8, da), F32),
-        vmem((8, da), F32),
+        vmem((2, 16, da // 2), BF16),
+        vmem((16, da // 2), BF16),
         dma((3, NX)), dma((3, NX)),
         dma((3, NX)), dma((3, NX)),
         dma((2, 3, NZ // 2)), dma((2, 3, NZ // 2)),

time: 56.1 us -> 55.4 us (0.988)
  Pallas kernels: 55.4 us -> 54.6 us
    pallas_call x1, Pallas kernels: 53.5 us -> 52.7 us  [shards(): pl.pallas_call(kernel, out_shape=(jax.ShapeDtypeStruct((vq.shape[0] // 4,...]
where the time goes in v5:
time: 55.4 us; the launch traced here: 55.3 us
  Pallas kernels  54.6 us (99%)
  between operations  0.64 us (1%)
    pallas_call x1, Pallas kernels, shards(): pl.pallas_call(kernel, out_shape=(jax.ShapeDtypeStruct((vq.shape[0] // 4,...  52.7 us
    pallas_call x1, Pallas kernels, shards(): pl.pallas_call(hand_over, out_shape=tuple((jax.ShapeDtypeStruct(o.shape,...  1.87 us

profile of v5, /device:TPU:1, one launch (start us, length us, event | category | flops | bytes accessed | tf_op | source)
XLA Modules:
  0.0 55.3 jit_solution(14791207490110505484)
XLA Ops:
  0.6 52.7 %shard_map.104 = (bf16[64,4096]{1,0:T(8,128)(2,1)}, bf16[8,2048]{1,0:T(8,128)(2,1)}) custom-call(s32[128]{0:T(128)} %ws.1, bf16[256,512]{1,0:T(8,128)(2,1)} %vq_in.1, bf16[256,512]{1,0:T(8,128)(2,1)} %vk_in.1, bf16[256,512]{1,0:T(8,128)(2,1)} %vv_in.1, bf16[32,512]{1,0:T(8,128)(2,1)} %aq_in.1, bf16[32,512]{1,0:T(8,128)(2,1)} %ak_in.1, ...), custom_call_target="tpu_custom_call" | custom-call | flops 3000000000 | bytes 16000000 | tf_op jit(solution)/shard_map/pallas_call | solution.py:532
  53.4 1.9 %shard_map.105 = (bf16[64,4096]{1,0:T(8,128)(2,1)}, bf16[8,2048]{1,0:T(8,128)(2,1)}) custom-call(bf16[64,4096]{1,0:T(8,128)(2,1)} %get-tuple-element.4.ov, bf16[8,2048]{1,0:T(8,128)(2,1)} %get-tuple-element.5.oa), custom_call_target="tpu_custom_call" | custom-call | tf_op jit(solution)/shard_map/pallas_call | solution.py:546

commit v6 on v5

--- a/solution.py
+++ b/solution.py
@@ -31,7 +31,7 @@
 def kernel(
     ws, vq_in, vk_in, vv_in, aq_in, ak_in, av_in, wv_in, wa_in, ov, oa,
     vq, vk, vv, aq, ak_flat, av_flat, wv, wa, kb, vo, va, po, pst, pr, prs, ao, aa, ysend, yrecv, yown, aown, asend, arecv,
-    s_pa, r_pa, s_pb, r_pb, s_z, r_z, s_f, r_f, s_vf, r_vf, s_w, r_w, s_vo, r_vo, s_p, r_p, s_ao, r_ao, s_y, r_y, s_ya, r_ya, l_w,
+    s_pa, r_pa, s_pb, r_pb, s_z, r_z, s_f, r_f, s_vf, r_vf, s_w, r_w, s_vo, r_vo, s_p, r_p, s_ao, r_ao, s_y, r_y, s_ya, r_ya, l_w, ov_held, l_o,
 ):
     seq, head = lax.axis_index("seq"), lax.axis_index("head")
     yh, x, z = seq // (NX * NZ), (seq // NZ) % NX, seq % NZ
@@ -464,11 +464,15 @@
     for drain in drains:
         drain()
 
+    def ov_copy(n):
+        at = pl.ds(pl.multiple_of(n * width, width), width)
+        return pltpu.make_async_copy(ov_held.at[n], ov.at[:, at], l_o.at[n])
+
     def finish(n, carry):
         for m in range(2):
             y_copy(n, m).wait_recv()
-        at = pl.ds(pl.multiple_of(n * width, width), width)
-        ov[:, at] = (yown[n] + yrecv[n].astype(F32)).astype(BF16)
+        ov_held[n] = (yown[n] + yrecv[n].astype(F32)).astype(BF16)
+        ov_copy(n).start()
         return carry
 
     lax.fori_loop(0, n_chunks, finish, 0)
@@ -477,13 +481,29 @@
     theirs = arecv[...].astype(F32)
     oa[...] = (aown[yl] + jnp.concatenate([theirs[:8], theirs[8:]], axis=1)).astype(BF16)
 
+    def written(n, carry):
+        ov_copy(n).wait()
+        return carry
+
+    lax.fori_loop(0, n_chunks, written, 0)
+
     last.wait_send()
     y_sent()
 
 
-def hand_over(ov, oa, to_v, to_a):
-    to_v[...] = ov[...]
-    to_a[...] = oa[...]
+def hand_over(ov, oa, to_v, to_a, tv, ta, sems):
+    rows = ov.shape[0] // 2
+    steps = [(ov.at[pl.ds(i * rows, rows)], tv.at[pl.ds(i * rows, rows)], to_v.at[pl.ds(i * rows, rows)]) for i in range(2)]
+    steps.append((oa, ta, to_a))
+    ins = [pltpu.make_async_copy(src, held, sems.at[0, i]) for i, (src, held, _) in enumerate(steps)]
+    outs = [pltpu.make_async_copy(held, dst, sems.at[1, i]) for i, (_, held, dst) in enumerate(steps)]
+    for copy in ins:
+        copy.start()
+    for arrived, leave in zip(ins, outs):
+        arrived.wait()
+        leave.start()
+    for copy in outs:
+        copy.wait()
 
 
 def shards(vq, vk, vv, aq, ak, av, ws, wv, wa):
@@ -527,6 +547,8 @@
         dma((2, n_chunks)), dma((2, n_chunks)),
         dma, dma,
         dma((2,)),
+        vmem((n_chunks, VB // 2, dv // n_chunks), BF16),
+        dma((n_chunks,)),
     ]
     any_spec = pl.BlockSpec(memory_space=pl.ANY)
     outs = pl.pallas_call(
@@ -536,7 +558,7 @@
             jax.ShapeDtypeStruct((aq.shape[0] // 4, da), BF16),
         ),
         in_specs=[pl.BlockSpec(memory_space=pltpu.SMEM)] + [any_spec] * 8,
-        out_specs=(pl.BlockSpec(memory_space=pltpu.VMEM), pl.BlockSpec(memory_space=pltpu.VMEM)),
+        out_specs=(any_spec, pl.BlockSpec(memory_space=pltpu.VMEM)),
         scratch_shapes=scratch,
         compiler_params=pltpu.CompilerParams(
             collective_id=0, has_side_effects=True, vmem_limit_bytes=60 * 1024 * 1024
@@ -544,7 +566,11 @@
         cost_estimate=pl.CostEstimate(flops=3_000_000_000, bytes_accessed=16_000_000, transcendentals=4_000_000),
     )(ws, vq, vk, vv, aq, ak, av, wv, wa)
     return pl.pallas_call(
-        hand_over, out_shape=tuple(jax.ShapeDtypeStruct(o.shape, o.dtype) for o in outs)
+        hand_over,
+        out_shape=tuple(jax.ShapeDtypeStruct(o.shape, o.dtype) for o in outs),
+        in_specs=[any_spec] * 2,
+        out_specs=(any_spec, any_spec),
+        scratch_shapes=[vmem(o.shape, o.dtype) for o in outs] + [dma((2, 3))],
     )(*outs)
 
 

time: 55.4 us -> 55.6 us (level)
  no operation moved by 1% of the time
where the time goes in v6:
time: 55.6 us; the launch traced here: 55.5 us
  Pallas kernels  54.8 us (99%)
  between operations  0.64 us (1%)
    pallas_call x1, Pallas kernels, shards(): pl.pallas_call(kernel, out_shape=(jax.ShapeDtypeStruct((vq.shape[0] // 4,...  53 us
    pallas_call x1, Pallas kernels, shards(): pl.pallas_call(hand_over, out_shape=tuple((jax.ShapeDtypeStruct(o.shape,...  1.79 us

profile of v6, /device:TPU:1, one launch (start us, length us, event | category | flops | bytes accessed | tf_op | source)
XLA Modules:
  0.0 55.5 jit_solution(14858937083449138558)
XLA Ops:
  0.6 53.0 %shard_map.104 = (bf16[64,4096]{1,0:T(8,128)(2,1)}, bf16[8,2048]{1,0:T(8,128)(2,1)}) custom-call(s32[128]{0:T(128)} %ws.1, bf16[256,512]{1,0:T(8,128)(2,1)} %vq_in.1, bf16[256,512]{1,0:T(8,128)(2,1)} %vk_in.1, bf16[256,512]{1,0:T(8,128)(2,1)} %vv_in.1, bf16[32,512]{1,0:T(8,128)(2,1)} %aq_in.1, bf16[32,512]{1,0:T(8,128)(2,1)} %ak_in.1, ...), custom_call_target="tpu_custom_call" | custom-call | flops 3000000000 | bytes 16000000 | tf_op jit(solution)/shard_map/pallas_call | solution.py:554
  53.7 1.8 %shard_map.105 = (bf16[64,4096]{1,0:T(8,128)(2,1)}, bf16[8,2048]{1,0:T(8,128)(2,1)}) custom-call(bf16[64,4096]{1,0:T(8,128)(2,1)} %get-tuple-element.4.ov, bf16[8,2048]{1,0:T(8,128)(2,1)} %get-tuple-element.5.oa), custom_call_target="tpu_custom_call" | custom-call | tf_op jit(solution)/shard_map/pallas_call | solution.py:568
